TPU v7x, 256 devices: a whole 4x4x8 slice. The times are simulated.
256 devices in a mesh: dp: 32 (over y, x, core), tensor: 8 (over z).
Axes of the slice: x: 4, y: 4, z: 8, core: 2. Of those that a mesh axis runs over, the one named last changes fastest.
Arguments:
- streams: bfloat16 [4, 8192, 5120], P(None, 'dp', 'tensor'), may hold values from -70 to 70
- stream_grads: bfloat16 [4, 8192, 5120], P(None, 'dp', 'tensor'), may hold values from -6 to 6
- branch_out: bfloat16 [8192, 5120], P('dp', 'tensor'), may hold values from -6 to 6
- query_grads: bfloat16 [8192, 5120], P('dp', 'tensor'), may hold values from -6 to 6
- query_weight: bfloat16 [5120, 5120], P(None, 'tensor'), may hold values from -0.078125 to 0.078125
- norm_gain: float32 [5120], P('tensor'), may hold values from 0.5 to 1.5
- coef_weight: bfloat16 [5120, 6], P('tensor'), may hold values from -0.078125 to 0.078125
- static_coef: float32 [4, 6], replicated, may hold values from -1 to 1
Outputs:
- streams_grad: bfloat16 [4, 8192, 5120], P(None, 'dp', 'tensor')
- branch_grad: bfloat16 [8192, 5120], P('dp', 'tensor')
- query_weight_grad: float32 [5120, 5120], P('dp', 'tensor')
- gain_grad: float32 [5120], P('tensor')
- coef_weight_grad: float32 [5120, 6], P('tensor')
- static_grad: float32 [4, 6], replicated
All inputs are finite; a program needn't handle non-finite values.
Results may differ from a plain program's by a relative error of at most 0.0029.
Values may be sent and summed in bfloat16 or wider, within the bound.
A program may use at most 128 MiB of HBM per device.

v0:
```python
import jax
import jax.numpy as jnp
from jax import lax
from jax.sharding import PartitionSpec as P

EPS = 1e-06
HIGH = lax.Precision.HIGHEST


def local(
    streams,
    stream_grads,
    branch_out,
    query_grads,
    query_weight,
    norm_gain,
    coef_weight,
    static_coef,
):
    model_width = query_weight.shape[0]
    stream_vals = streams.astype(jnp.float32)
    grad_vals = stream_grads.astype(jnp.float32)
    branch_vals = branch_out.astype(jnp.float32)
    coef_w = coef_weight.astype(jnp.float32)
    projected = jnp.einsum("itd,dc->tic", stream_vals, coef_w, precision=HIGH)
    depth_part = jnp.einsum("td,jtd->tj", branch_vals, grad_vals, precision=HIGH)
    route_part = jnp.einsum("itd,jtd->tij", stream_vals, grad_vals, precision=HIGH)
    sum_part = jnp.einsum("itd,itd->ti", stream_vals, stream_vals, precision=HIGH)
    sum_sq, projected = lax.psum((sum_part, projected), "tensor")
    inv_rms = lax.rsqrt(sum_sq / model_width + EPS)
    squashed = jnp.tanh(inv_rms[:, :, None] * projected)
    coeffs = static_coef[None] + squashed
    depth_coef = coeffs[:, :, 0]
    width_coef = coeffs[:, :, 1]
    route_coef = coeffs[:, :, 2:]
    mixed = jnp.einsum("ti,itd->td", width_coef, stream_vals, precision=HIGH)
    mixed_sq = lax.psum(jnp.sum(mixed * mixed, axis=-1), "tensor")
    mix_inv = lax.rsqrt(mixed_sq / model_width + EPS)
    normed = (mixed * mix_inv[:, None] * norm_gain[None]).astype(jnp.bfloat16)
    branch_grad = jnp.einsum("tj,jtd->td", depth_coef, grad_vals, precision=HIGH).astype(
        jnp.bfloat16
    )
    depth_grad, route_grad = lax.psum((depth_part, route_part), "tensor")
    direct = jnp.einsum("tij,jtd->itd", route_coef, grad_vals, precision=HIGH)
    gathered = lax.all_gather(normed, "tensor", axis=1, tiled=True)
    weight_grad = lax.psum_scatter(
        lax.dot_general(
            gathered, query_grads, (((0,), (0,)), ((), ())), preferred_element_type=jnp.float32
        ),
        "dp",
        scatter_dimension=0,
        tiled=True,
    )
    norm_grad = lax.psum_scatter(
        lax.dot_general(
            query_weight, query_grads, (((1,), (1,)), ((), ())), preferred_element_type=jnp.float32
        ),
        "tensor",
        scatter_dimension=0,
        tiled=True,
    ).T
    gain_part = jnp.sum(norm_grad * mixed * mix_inv[:, None], axis=0)
    scaled_grad = norm_grad * norm_gain[None]
    inner_sum = lax.psum(jnp.sum(scaled_grad * mixed, axis=-1), "tensor")
    mixed_grad = (
        mix_inv[:, None] * scaled_grad - mixed * (mix_inv**3 * inner_sum / model_width)[:, None]
    )
    mix_grad = lax.psum(jnp.einsum("itd,td->ti", stream_vals, mixed_grad, precision=HIGH), "tensor")
    coef_grad = jnp.concatenate([depth_grad[:, :, None], mix_grad[:, :, None], route_grad], axis=-1)
    pre_grad = coef_grad * (1.0 - squashed * squashed)
    proj_grad = pre_grad * inv_rms[:, :, None]
    scale_grad = jnp.sum(pre_grad * projected, axis=-1)
    coef_part = jnp.einsum("itd,tic->dc", stream_vals, proj_grad, precision=HIGH)
    static_part = jnp.sum(coef_grad, axis=0)
    gain_grad, coef_wgrad, static_grad = lax.psum((gain_part, coef_part, static_part), "dp")
    stream_out = direct + width_coef.T[:, :, None] * mixed_grad[None]
    stream_out = stream_out + jnp.einsum("tic,dc->itd", proj_grad, coef_w, precision=HIGH)
    stream_out = stream_out - (scale_grad * inv_rms**3 / model_width).T[:, :, None] * stream_vals
    return (
        stream_out.astype(jnp.bfloat16),
        branch_grad,
        weight_grad,
        gain_grad,
        coef_wgrad,
        static_grad,
    )


def solution(mesh):
    in_specs = (
        P(None, "dp", "tensor"),
        P(None, "dp", "tensor"),
        P("dp", "tensor"),
        P("dp", "tensor"),
        P(None, "tensor"),
        P("tensor"),
        P("tensor", None),
        P(),
    )
    out_specs = (
        P(None, "dp", "tensor"),
        P("dp", "tensor"),
        P("dp", "tensor"),
        P("tensor"),
        P("tensor", None),
        P(),
    )
    return jax.shard_map(local, mesh=mesh, in_specs=in_specs, out_specs=out_specs, check_vma=False)
```

profile of v0, /device:TPU:1, one launch (start us, length us, event | category | flops | bytes accessed | tf_op | source)
XLA Modules:
  0.0 336.1 jit_solution(8051599126885413675)
XLA Ops:
  7.2 0.0 copy-start
  7.2 0.0 reduce-scatter.3.cloned.1.call-start
  7.2 7.5 %fusion.30 = f32[5120,256]{1,0:T(8,128)} fusion(bf16[5120,640]{1,0:T(8,128)(2,1)} %param.12, bf16[256,640]{1,0:T(8,128)(2,1)} %param.11), kind=kOutput, calls=%fused_computation.54 | convolution fusion | flops 1677721600 | bytes 12124160 | tf_op jit(solution)/shard_map/dot_general | solution.py:55
  14.7 0.0 copy-start.1
  14.7 0.0 reduce-scatter.3.cloned.1.call-update
  14.8 0.0 copy-start.5
  14.8 0.0 copy-start.7
  14.8 0.0 all-gather.2.cloned.1.call-start
  14.8 1.2 copy-done.1
  16.1 0.3 fusion
  16.4 0.0 copy-done.5
  16.4 0.4 convolution_bitcast_fusion
  16.8 29.7 %all-reduce.2 = (f32[256,4]{0,1:T(4,128)S(1)}, f32[256,4,6]{0,2,1:T(8,128)S(1)}) all-reduce(f32[256,4]{0,1:T(4,128)S(1)} %fusion, f32[256,4,6]{0,2,1:T(8,128)S(1)} %convolution_bitcast_fusion), channel_id=1, replica_groups=mesh['dp'=32,'tensor'=8] {'tensor'}, use_global_device_ids=true, to_apply=%region_0.0 | all-reduce | flops 7168 | bytes 57344 | tf_op jit(solution)/shard_map/psum | solution.py:29
  46.5 0.0 copy-done.7
  46.5 0.1 fusion.18
  46.6 1.1 fusion.1
  47.8 0.0 copy-start.6
  47.8 1.3 copy.34
  49.1 0.1 multiply_reduce_fusion.2
  49.2 13.3 %psum.72 = f32[256]{0:T(256)S(1)} all-reduce(f32[256]{0:T(256)S(1)} %multiply_reduce_fusion.2), channel_id=1, replica_groups=mesh['dp'=32,'tensor'=8] {'tensor'}, use_global_device_ids=true, to_apply=%region_3.0 | all-reduce | flops 256 | bytes 2048 | tf_op jit(solution)/shard_map/psum | solution.py:37
  62.5 22.8 %reduce-scatter.3.cloned.1.call-done = f32[640,256]{1,0:T(8,128)} async-done(((f32[5120,256]{1,0:T(8,128)}), f32[640,256]{1,0:T(8,128)}) %reduce-scatter.3.cloned.1.call-update) | async-done | bytes 655376 | tf_op jit(solution)/shard_map/reduce_scatter | solution.py:54
  85.3 0.0 copy-done.6
  85.3 1.4 fusion.7
  86.7 11.8 %psum.73 = f32[256]{0:T(256)S(1)} all-reduce(f32[256]{0:T(256)S(1)} %get-tuple-element.13), channel_id=1, replica_groups=mesh['dp'=32,'tensor'=8] {'tensor'}, use_global_device_ids=true, to_apply=%region_6.0 | all-reduce | flops 256 | bytes 2048 | tf_op jit(solution)/shard_map/psum | solution.py:64
  98.5 2.3 multiply_convert_fusion
  100.8 0.0 all-gather.2.cloned.1.call-update
  100.8 0.2 reduce-scatter.5.cloned.1.call-start
  101.0 42.3 %all-gather.2.cloned.1.call-done = bf16[256,5120]{0,1:T(8,128)(2,1)} async-done(((bf16[256,640]{0,1:T(8,128)(2,1)}), bf16[256,5120]{0,1:T(8,128)(2,1)}) %all-gather.2.cloned.1.call-update) | async-done | bytes 2621456 | tf_op jit(solution)/shard_map/all_gather | solution.py:45
  143.4 8.6 %fusion.31 = f32[5120,640]{1,0:T(8,128)} fusion(bf16[256,5120]{0,1:T(8,128)(2,1)} %all-gather.2.cloned.1.call-done, bf16[256,640]{1,0:T(8,128)(2,1)} %param.11), kind=kOutput, calls=%fused_computation.55 | convolution fusion | flops 1677721600 | bytes 16056320 | tf_op jit(solution)/shard_map/dot_general | solution.py:47
  152.0 0.0 reduce-scatter.5.cloned.1.call-update
  152.0 0.0 copy-done
  152.0 1.9 fusion.4
  153.9 0.2 copy.20
  154.1 2.8 fusion.8
  156.9 0.1 copy.36
  157.0 0.1 copy.16
  157.1 1.1 copy.14
  158.2 0.1 copy.44
  158.4 3.7 %fusion.10 = bf16[256,1,640]{2,1,0:T(2,128)(2,1)S(1)} fusion(f32[256,4,1]{1,2,0:T(1,128)S(1)} %bitcast.66, bf16[4,256,640]{2,1,0:T(8,128)(2,1)S(1)} %copy-done), kind=kOutput, calls=%fused_computation.24 | convolution fusion | flops 7864320 | bytes 1642496 | tf_op jit(solution)/shard_map/tj,jtd->td/dot_general | solution.py:40
  162.0 0.0 copy-start.2
  162.0 0.8 copy.64
  162.8 0.4 copy-done.2
  163.2 1.1 copy.17
  164.3 1.4 multiply_reduce_fusion
  165.8 21.8 %all-reduce.1 = (f32[256,4,4]{0,2,1:T(4,128)S(1)}, f32[256,4,1]{0,2,1:T(1,128)S(1)}, f32[256,4,1]{0,2,1:T(1,128)S(1)}) all-reduce(f32[256,4,4]{0,2,1:T(4,128)S(1)} %copy.20, f32[256,4,1]{0,2,1:T(1,128)S(1)} %broadcast_in_dim.5, f32[256,4,1]{0,2,1:T(1,128)S(1)} %broadcast_in_dim.4), channel_id=1, replica_groups=mesh['dp'=32,'tensor'=8] {'tensor'}, use_global_device_ids=true, to_apply=%region_9.0 | all-reduce | flops 6144 | bytes 49152 | tf_op jit(solution)/shard_map/psum | solution.py:43
  187.5 0.1 fusion.19
  187.6 0.1 copy.22
  187.8 0.0 copy-start.3
  187.8 0.0 copy-start.4
  187.8 1.5 fusion.16
  189.3 0.0 copy-done.3
  189.3 0.0 copy-done.4
  189.3 7.5 %fusion.3 = bf16[4,256,640]{2,0,1:T(4,128)(2,1)S(1)} fusion(f32[256,4,640]{2,0,1:T(8,128)S(1)} %fusion.16, f32[256,4,4]{2,1,0:T(4,128)S(1)} %copy-done.4, f32[4,256]{0,1:T(8,128)S(1)} %copy.22, f32[256,640]{1,0:T(8,128)S(1)} %copy-done.3, f32[4,256]{0,1:T(8,128)S(1)} %copy.16, bf16[4,256,640]{2,1,0:T(8,128)(2,1)S(1)} %copy-done.1, ...), kind=kOutput, calls=%fused_computation.6 | convolution fusion | flops 36044800 | bytes 7233536 | tf_op jit(solution)/shard_map/tij,jtd->itd/dot_general | solution.py:44
  196.8 1.2 copy.24
  198.1 0.6 convolution_bitcast_fusion.1
  198.7 130.9 %all-reduce = (f32[640]{0:T(1024)}, f32[640,6]{0,1:T(8,128)}, f32[4,6]{1,0:T(4,128)}) all-reduce(f32[640]{0:T(1024)S(1)} %get-tuple-element.12, f32[640,6]{0,1:T(8,128)S(1)} %convolution_bitcast_fusion.1, f32[4,6]{1,0:T(4,128)S(1)} %get-tuple-element.14), channel_id=1, replica_groups=mesh['dp'=32,'tensor'=8] {'dp'}, use_global_device_ids=true, to_apply=%region_13.0 | all-reduce | flops 4504 | bytes 36032 | tf_op jit(solution)/shard_map/psum | solution.py:75
  329.6 0.0 reduce-scatter.5.cloned.1.call-done
  (9 shorter events, 0.1 us)
Async XLA Ops:
  7.2 144.9 %copy-start = (bf16[4,256,640]{2,1,0:T(8,128)(2,1)S(1)}, bf16[4,256,640]{2,1,0:T(8,128)(2,1)}, u32[]{:S(2)}) copy-start(bf16[4,256,640]{2,1,0:T(8,128)(2,1)} %param.9) | copy-start | bytes 3932164
  7.2 78.1 %reduce-scatter.3.cloned.1.call-start = ((), (), s32[]{:S(2)}) async-start(), calls=%async_computation.2 | async-start | bytes 5898240 | tf_op jit(solution)/shard_map/reduce_scatter | solution.py:54
  14.7 1.3 copy-start.1
  14.8 1.6 copy-start.5
  14.8 31.8 %copy-start.7 = (f32[4,6]{1,0:T(4,128)S(1)}, f32[4,6]{1,0:T(4,128)}, u32[]{:S(2)}) copy-start(f32[4,6]{1,0:T(4,128)} %param.15) | copy-start | bytes 292
  14.8 128.6 %all-gather.2.cloned.1.call-start = ((), (), s32[]{:S(2)}) async-start(), calls=%async_computation.3 | async-start | bytes 2949120 | tf_op jit(solution)/shard_map/all_gather | solution.py:45
  47.8 37.5 %copy-start.6 = (f32[640]{0:T(1024)S(1)}, f32[640]{0:T(1024)}, u32[]{:S(2)}) copy-start(f32[640]{0:T(1024)} %param.13) | copy-start | bytes 7684
  100.8 228.8 %reduce-scatter.5.cloned.1.call-start = ((), (), s32[]{:S(2)}) async-start(), calls=%async_computation.4 | async-start | bytes 13516800 | tf_op jit(solution)/shard_map/reduce_scatter | solution.py:46
  162.0 1.2 copy-start.2
  187.8 1.5 copy-start.3
  187.8 1.5 copy-start.4
Sparse Core Ops, SparseCore 0:
  14.9 70.3 reduce-scatter.2
  100.9 42.3 all-gather.1
  152.1 114.0 reduce-scatter.4
where the time goes:
time: 339 us; the launch traced here: 336 us
  blocking collectives  207 us (61%)
  waiting for transfers between devices  65.2 us (19%)
  matrix products  34.5 us (10%)
  between operations  13.9 us (4%)
  local copies, waits for them, and re-layouts  7.93 us (2%)
  other arithmetic  6.88 us (2%)
    psum x1, blocking collectives, local(): lax.psum((gain_part, coef_part, static_part), 'dp')  131 us
    all_gather x1, waiting for transfers between devices, local(): gathered = lax.all_gather(normed, 'tensor', axis=1, tiled=True)  42.3 us
    psum x1, blocking collectives, local(): sum_sq, projected = lax.psum((sum_part, projected), 'tensor')  29.7 us
    reduce_scatter x1, waiting for transfers between devices, local(): lax.psum_scatter(lax.dot_general(query_weight, query_grads, (((1,), (1,))...  22.8 us
    psum x1, blocking collectives, local(): depth_grad, route_grad = lax.psum((depth_part, route_part), 'tensor')  21.8 us
    psum x1, blocking collectives, local(): mixed_sq = lax.psum(jnp.sum(mixed * mixed, axis=-1), 'tensor')  13.3 us
    psum x1, blocking collectives, local(): inner_sum = lax.psum(jnp.sum(scaled_grad * mixed, axis=-1), 'tensor')  11.8 us
    dot_general x1, matrix products, local(): lax.dot_general(gathered, query_grads, (((0,), (0,)), ((), ())), preferre...  8.63 us
  transfers between devices with their start and end apart: 3, of which 2 were waited for; matrix products, arithmetic and copies ran while one was open for 8% of the time, Pallas kernels for 0%

commit v1 on v0

v1 whole, which is shorter than its diff:
```python
import functools

import jax
import jax.numpy as jnp
from jax import lax
from jax.experimental import pallas as pl
from jax.experimental.pallas import tpu as pltpu
from jax.sharding import PartitionSpec as P

EPS = 1e-06
MESH = pl.DeviceIdType.MESH
F32 = jnp.float32
BF16 = jnp.bfloat16

T = 256
F = 640
NZ = 8
D = F * NZ
RB = 160
HB = RB // 2
NX = 4
NY = 4


def dot_nt(a, b):
    return lax.dot_general(a, b, (((1,), (1,)), ((), ())), preferred_element_type=F32)


def dot_nn(a, b):
    return lax.dot_general(a, b, (((1,), (0,)), ((), ())), preferred_element_type=F32)


def split3(v):
    hi = v.astype(BF16).astype(F32)
    rest = v - hi
    mid = rest.astype(BF16).astype(F32)
    return hi, mid, (rest - mid).astype(BF16).astype(F32)


def kernel(
    s_h, g_h, b_h, q_h, w_h, gain, cw, st,
    so_h, bo_h, wo_h, gain_o, cw_o, st_o,
    xs, gs, qq, wbuf,
    pbuf, rs_send, rs_recv,
    cl, r1, cfull, hbuf,
    mixed, nts, nbuf, col1, col2, cwx,
    xsend, xrecv, keep, xa, wo_v,
    so_v, bo_v, acc, sb, sc, sx, sy,
    in_sem, win_sem, out_sem,
    rs_ss, rs_rs, ag_ss, ag_rs, sync_ss, sync_rs, core_ss, core_rs, x_ss, x_rs, sm_ss, sm_rs,
):
    dp = lax.axis_index("dp")
    z = lax.axis_index("tensor")
    core = lax.rem(dp, 2)
    x = lax.rem(dp // 2, NX)
    y = dp // (2 * NX)

    def zdev(k):
        return (dp, lax.rem(z + k + NZ, NZ))

    def xdev(k):
        return ((y * NX + lax.rem(x + k + NX, NX)) * 2 + core, z)

    def ydev(k):
        return ((lax.rem(y + k + NY, NY) * NX + x) * 2 + core, z)

    cdev = (dp + 1 - 2 * core, z)

    def rcopy(src, dst, ss, rs, dev):
        return pltpu.make_async_remote_copy(
            src_ref=src, dst_ref=dst, send_sem=ss, recv_sem=rs, device_id=dev, device_id_type=MESH
        )

    q_in = pltpu.make_async_copy(q_h, qq.at[core], in_sem.at[0])
    s_in = pltpu.make_async_copy(s_h, xs.at[0:4], in_sem.at[1])
    g_in = pltpu.make_async_copy(g_h, gs, in_sem.at[2])
    b_in = pltpu.make_async_copy(b_h, xs.at[4], in_sem.at[3])

    def w_in(k):
        blk = lax.rem(z + k, NZ)
        return pltpu.make_async_copy(
            w_h.at[pl.ds(pl.multiple_of(blk * F, F), F)], wbuf.at[k], win_sem.at[k]
        )

    q_in.start()
    w_in(4).start()
    s_in.start()
    g_in.start()
    b_in.start()
    for k in (3, 5, 2, 6, 1, 7, 0):
        w_in(k).start()

    barrier = pltpu.get_barrier_semaphore()
    peers = [zdev(k) for k in range(1, NZ)] + [xdev(k) for k in (1, 2, 3)]
    peers += [ydev(k) for k in (1, 2, 3)] + [cdev]
    for dev in peers:
        pl.semaphore_signal(barrier, inc=1, device_id=dev, device_id_type=MESH)

    def rs_partial(k):
        w_in(k).wait()
        pbuf[k] = dot_nt(qq[core], wbuf[k])

    RIGHT, LEFT = 0, 1
    HALF = T // 2

    def rs_copy(way, step, half):
        return rcopy(
            rs_send.at[way, step, half],
            rs_recv.at[way, step, half],
            rs_ss.at[way, step, half],
            rs_rs.at[way, step, half],
            zdev(1 if way == RIGHT else -1),
        )

    def rs_block(way, step):
        return 4 - step if way == RIGHT else 4 + step if step else 4

    def rs_raw(way, step, half):
        rs_send[way, step, half] = pbuf[rs_block(way, step), half * HALF : (half + 1) * HALF].astype(BF16)
        rs_copy(way, step, half).start()

    def rs_add(way, step, half):
        rs_copy(way, step - 1, half).wait_recv()
        v = pbuf[rs_block(way, step), half * HALF : (half + 1) * HALF]
        rs_send[way, step, half] = (v + rs_recv[way, step - 1, half].astype(F32)).astype(BF16)
        rs_copy(way, step, half).start()

    q_in.wait()
    rs_partial(4)
    pl.semaphore_wait(barrier, len(peers))
    rs_raw(RIGHT, 0, 0)
    rs_raw(LEFT, 0, 1)
    q_swap = rcopy(qq.at[core], qq.at[core], core_ss.at[0], core_rs.at[0], cdev)
    q_swap.start()
    rs_partial(3)
    rs_raw(RIGHT, 1, 1)
    rs_partial(5)
    rs_raw(LEFT, 1, 0)

    s_in.wait()
    g_in.wait()
    b_in.wait()
    cw8 = jnp.concatenate([cw[...].astype(F32), jnp.zeros((10, F), F32)], axis=0).astype(BF16)
    rows_i = lax.broadcasted_iota(jnp.int32, (128, 128), 0)
    cols_i = lax.broadcasted_iota(jnp.int32, (128, 128), 1)
    eye = rows_i == cols_i

    def diag(block):
        return jnp.sum(jnp.where(eye, block, 0.0), axis=0, keepdims=True)

    def gram(blk, carry):
        at = pl.ds(pl.multiple_of(blk * 128, 128), 128)
        sb_blk = xs[:, at, :].reshape(5 * 128, F)
        g_blk = gs[:, at, :].reshape(4 * 128, F)
        sg = dot_nt(sb_blk, g_blk)
        route = [
            [diag(sg[i * 128 : i * 128 + 128, j * 128 : j * 128 + 128]) for j in range(4)] for i in range(5)
        ]
        s_blk = sb_blk[: 4 * 128]
        ss = dot_nt(s_blk, s_blk)
        gr = {
            (i, j): diag(ss[i * 128 : i * 128 + 128, j * 128 : j * 128 + 128])
            for i in range(4)
            for j in range(i, 4)
        }
        proj = dot_nt(cw8, s_blk)
        zero = jnp.zeros((1, 128), F32)
        for i in range(4):
            cl[i, :, at] = jnp.concatenate(
                [proj[0:6, i * 128 : i * 128 + 128], gr[i, i], route[4][i]], axis=0
            )
        for half in range(2):
            cl[4 + half, :, at] = jnp.concatenate(
                [route[2 * half + i][j] for i in range(2) for j in range(4)], axis=0
            )
        cl[6, :, at] = jnp.concatenate(
            [gr[0, 1], gr[0, 2], gr[0, 3], gr[1, 2], gr[1, 3], gr[2, 3], zero, zero], axis=0
        )
        cl[7, :, at] = jnp.zeros((8, 128), F32)
        return carry

    lax.fori_loop(0, 2, gram, 0)

    def sync_out(k):
        return rcopy(
            cl.at[lax.rem(z + k, NZ)], r1.at[k], sync_ss.at[0, k], sync_rs.at[0, k], zdev(k)
        )

    def sync_back(k):
        return rcopy(cfull.at[z], cfull.at[z], sync_ss.at[1, k], sync_rs.at[1, k], zdev(k))

    def sync_back_in(k):
        at = cfull.at[lax.rem(z - k + NZ, NZ)]
        return rcopy(at, at, sync_ss.at[1, k], sync_rs.at[1, k], zdev(k))

    for k in range(1, NZ):
        sync_out(k).start()

    rs_partial(2)
    rs_partial(6)
    rs_add(RIGHT, 1, 0)
    rs_add(LEFT, 1, 1)

    total = cl[z]
    for k in range(1, NZ):
        sync_out(k).wait_recv()
        total = total + r1[k]
    cfull[z] = total
    for k in range(1, NZ):
        sync_back(k).start()

    rs_add(RIGHT, 2, 1)
    rs_add(LEFT, 2, 0)
    rs_partial(1)
    rs_partial(7)
    rs_partial(0)

    cw_f = cw8[0:8].astype(F32)
    for i in range(4):
        parts = [cw_f, cw_f, cw_f]
        if i:
            parts = [jnp.zeros((i * 32, F), F32)] + parts
        parts = parts + [jnp.zeros((128 - i * 32 - 24, F), F32)]
        cwx[i] = jnp.concatenate(parts, axis=0).astype(BF16)

    for k in range(1, NZ):
        sync_back_in(k).wait_recv()

    row8 = lax.broadcasted_iota(jnp.int32, (8, T), 0)

    def coefficients():
        proj, inv, sq, cf = [], [], [], []
        for i in range(4):
            piece = cfull[i]
            p8 = jnp.where(row8 < 6, piece, 0.0)
            iv = lax.rsqrt(piece[6:7] / D + EPS)
            th = jnp.tanh(iv * p8)
            stc = jnp.zeros((8, T), F32)
            for c in range(6):
                stc = jnp.where(row8 == c, st[i, c], stc)
            proj.append(p8)
            inv.append(iv)
            sq.append(th)
            cf.append(stc + th)
        off = cfull[6]
        at = {(0, 1): 0, (0, 2): 1, (0, 3): 2, (1, 2): 3, (1, 3): 4, (2, 3): 5}

        def g_of(i, j):
            if i == j:
                return cfull[i][6:7]
            r = at[min(i, j), max(i, j)]
            return off[r : r + 1]

        wid = [cf[i][1:2] for i in range(4)]
        gw = [sum(g_of(i, j) * wid[j] for j in range(4)) for i in range(4)]
        mixed_sq = sum(wid[i] * gw[i] for i in range(4))
        mix_inv = lax.rsqrt(mixed_sq / D + EPS)
        return proj, inv, sq, cf, wid, gw, mix_inv

    _, _, _, cf, _, _, mix_inv = coefficients()
    rows = jnp.concatenate(cf + [jnp.broadcast_to(mix_inv, (8, T)), jnp.zeros((88, T), F32)], axis=0)
    col1[...] = rows.T

    def mix(blk, carry):
        at = pl.ds(pl.multiple_of(blk * 32, 32), 32)
        c = col1[at, :]
        m = c[:, 1:2] * xs[0, at, :].astype(F32)
        for i in range(1, 4):
            m = m + c[:, 8 * i + 1 : 8 * i + 2] * xs[i, at, :].astype(F32)
        mixed[at, :] = m
        acc[0, at, :] = m * c[:, 32:33] * gain[...]
        return carry

    lax.fori_loop(0, T // 32, mix, 0)
    for k in range(4):
        pass
    for lane in range(F // 128):
        tr = acc[0, :, lane * 128 : lane * 128 + 128].T.astype(BF16)
        nts[lane * 128 : lane * 128 + 128, :] = tr

    def n_swap(kk):
        return rcopy(
            nts.at[pl.ds(pl.multiple_of((2 * kk + 1 - core) * RB, 32), RB)],
            nbuf.at[z, kk, core],
            core_ss.at[1 + kk],
            core_rs.at[1 + kk],
            cdev,
        )

    def n_swap_in(kk):
        return rcopy(
            nts.at[pl.ds(pl.multiple_of((2 * kk + 1 - core) * RB, 32), RB)],
            nbuf.at[z, kk, 1 - core],
            core_ss.at[1 + kk],
            core_rs.at[1 + kk],
            cdev,
        )

    for kk in range(2):
        n_swap(kk).start()
    for kk in range(2):
        nbuf[z, kk, core] = nts[pl.ds(pl.multiple_of((2 * kk + core) * RB, 32), RB), :]

    rs_add(RIGHT, 2, 0)
    rs_add(LEFT, 2, 1)

    def ag_copy(way, step, kk):
        blk = lax.rem(z - step + 1 + NZ, NZ) if way == RIGHT else lax.rem(z + step - 1, NZ)
        at = nbuf.at[blk, kk]
        return rcopy(at, at, ag_ss.at[way, step, kk], ag_rs.at[way, step, kk], zdev(1 if way == RIGHT else -1))

    def ag_in(way, step, kk):
        blk = lax.rem(z - step + NZ, NZ) if way == RIGHT else lax.rem(z + step, NZ)
        at = nbuf.at[blk, kk]
        return rcopy(at, at, ag_ss.at[way, step, kk], ag_rs.at[way, step, kk], zdev(1 if way == RIGHT else -1))

    for kk in range(2):
        n_swap_in(kk).wait_recv()
        ag_copy(RIGHT, 1, kk).start()
        ag_copy(LEFT, 1, kk).start()

    def ag_forward(step):
        for kk in range(2):
            for way in (RIGHT, LEFT):
                ag_in(way, step - 1, kk).wait_recv()
                if step < 4 or kk == way:
                    ag_copy(way, step, kk).start()

    par = lax.rem(z, 2)
    z0 = z - par
    q_swap_in = rcopy(qq.at[1 - core], qq.at[1 - core], core_ss.at[0], core_rs.at[0], cdev)
    q_swap_in.wait_recv()

    def pair_base(m):
        if m == 0:
            return z0
        if m == 3:
            return lax.rem(z0 + 4, NZ)
        sign = -1 if m == 1 else 1
        return lax.rem(z0 + sign * 2 * (1 - 2 * par) + NZ, NZ)

    def wg_block(m, r):
        xd = lax.rem(x + r, NX)
        n = nbuf.at[lax.rem(pair_base(m) + xd // 2, NZ), lax.rem(xd, 2)]
        return dot_nn(n[0], qq[0]) + dot_nn(n[1], qq[1])

    def red_copy(e, way, part):
        dev = (xdev if e < 4 else ydev)(1 if way == RIGHT else -1)
        return rcopy(
            xsend.at[e, way, part], xrecv.at[e, way, part], x_ss.at[e, way, part], x_rs.at[e, way, part], dev
        )

    def red_start(e, block):
        far = block(2).astype(BF16)
        xsend[e, RIGHT, 0] = far[:HB]
        red_copy(e, RIGHT, 0).start()
        xsend[e, LEFT, 0] = far[HB:]
        red_copy(e, LEFT, 0).start()
        near = block(1)
        xsend[e, RIGHT, 1] = near[HB:].astype(BF16)
        red_copy(e, RIGHT, 1).start()
        keep[e, RIGHT] = near[:HB]
        near = block(3)
        xsend[e, LEFT, 1] = near[:HB].astype(BF16)
        red_copy(e, LEFT, 1).start()
        keep[e, LEFT] = near[HB:]

    def red_forward(e):
        for way in (RIGHT, LEFT):
            red_copy(e, way, 0).wait_recv()
            xsend[e, way, 2] = (keep[e, way] + xrecv[e, way, 0].astype(F32)).astype(BF16)
            red_copy(e, way, 2).start()

    def red_finish(e, own):
        for way in (RIGHT, LEFT):
            for part in (1, 2):
                red_copy(e, way, part).wait_recv()
        top = own[:HB] + xrecv[e, RIGHT, 2].astype(F32) + xrecv[e, LEFT, 1].astype(F32)
        low = own[HB:] + xrecv[e, RIGHT, 1].astype(F32) + xrecv[e, LEFT, 2].astype(F32)
        return top, low

    def pair_start(m):
        red_start(m, functools.partial(wg_block, m))
        xa[pair_base(m) // 2] = wg_block(m, 0)

    def pair_finish(m):
        at = pair_base(m) // 2
        top, low = red_finish(m, xa[at])
        xa[at, :HB] = top
        xa[at, HB:] = low

    def branch(blk, carry):
        at = pl.ds(pl.multiple_of(blk * 32, 32), 32)
        c = col1[at, :]
        v = c[:, 0:1] * gs[0, at, :].astype(F32)
        for j in range(1, 4):
            v = v + c[:, 8 * j : 8 * j + 1] * gs[j, at, :].astype(F32)
        bo_v[at, :] = v.astype(BF16)
        return carry

    rs_add(RIGHT, 3, 1)
    rs_add(LEFT, 3, 0)
    lax.fori_loop(0, T // 32, branch, 0)
    bo_out = pltpu.make_async_copy(bo_v, bo_h, out_sem.at[0])
    bo_out.start()
    rs_add(RIGHT, 3, 0)
    rs_add(LEFT, 3, 1)

    ag_forward(2)
    pair_start(0)

    for way in (RIGHT, LEFT):
        for half in range(2):
            rs_copy(way, 3, half).wait_recv()

    def norm(blk, gain_sum):
        at = pl.ds(pl.multiple_of(blk * 128, 128), 128)
        ng = pbuf[0, at, :] + rs_recv[RIGHT, 3, blk].astype(F32) + rs_recv[LEFT, 3, blk].astype(F32)
        gain_sum = gain_sum + jnp.sum(ng * (mixed[at, :] * col1[at, 32:33]), axis=0, keepdims=True)
        scaled = ng * gain[...]
        pbuf[0, at, :] = scaled
        hi, mid, lo = split3(scaled)
        parts = jnp.concatenate([hi, mid, lo], axis=0).astype(BF16)
        prod = dot_nt(xs[0:4, at, :].reshape(4 * 128, F), parts)
        h = []
        for i in range(4):
            p = prod[i * 128 : i * 128 + 128]
            h.append(diag(p[:, 0:128] + p[:, 128:256] + p[:, 256:384]))
        hbuf[z, :, at] = jnp.concatenate(h + [jnp.zeros((4, 128), F32)], axis=0)
        return gain_sum

    gain_part = lax.fori_loop(0, T // 128, norm, jnp.zeros((1, F), F32))

    def h_out(k):
        return rcopy(hbuf.at[z], hbuf.at[z], sync_ss.at[2, k], sync_rs.at[2, k], zdev(k))

    def h_in(k):
        at = hbuf.at[lax.rem(z - k + NZ, NZ)]
        return rcopy(at, at, sync_ss.at[2, k], sync_rs.at[2, k], zdev(k))

    for k in range(1, NZ):
        h_out(k).start()

    red_forward(0)
    ag_forward(3)
    pair_start(1)

    for k in range(1, NZ):
        h_in(k).wait_recv()

    proj, inv, sq, cf, wid, gw, mix_inv = coefficients()
    h8 = hbuf[0]
    for k in range(1, NZ):
        h8 = h8 + hbuf[k]
    inner = sum(wid[i] * h8[i : i + 1] for i in range(4))
    kfac = mix_inv * mix_inv * mix_inv * inner / D
    rows, left, stat = [], [], []
    for i in range(4):
        mix_grad = mix_inv * h8[i : i + 1] - kfac * gw[i]
        route = cfull[4 + i // 2][4 * (i % 2) : 4 * (i % 2) + 4]
        cg = jnp.concatenate([cfull[i][7:8], mix_grad, route, jnp.zeros((2, T), F32)], axis=0)
        pre = cg * (1.0 - sq[i] * sq[i])
        pg = pre * inv[i]
        scale = jnp.sum(pre * proj[i], axis=0, keepdims=True) * (inv[i] * inv[i] * inv[i] / D)
        hi, mid, lo = split3(pg)
        left.append(jnp.concatenate([hi, mid, lo], axis=0))
        rows += [hi, mid, lo, wid[i], scale, cf[i][2:6], mix_inv, kfac]
        stat.append(jnp.broadcast_to(jnp.sum(cg, axis=1, keepdims=True), (8, 128)))
    col2[...] = jnp.concatenate(rows, axis=0).T
    cpart = dot_nn(jnp.concatenate(left, axis=1).astype(BF16), xs[0:4].reshape(4 * T, F))
    cpart = cpart[0:8] + cpart[8:16] + cpart[16:24]
    sb[0:8, :] = jnp.concatenate([cpart[0:6], gain_part, jnp.zeros((1, F), F32)], axis=0)
    sb[8:16, :] = jnp.concatenate(stat + [jnp.zeros((8, 128), F32)], axis=1)

    sm_core = rcopy(sb, sc, sm_ss.at[0], sm_rs.at[0], cdev)
    sm_core.start()

    lhs = col2[...].astype(BF16)
    for i in range(4):
        acc[i] = dot_nn(lhs, cwx[i])

    def out_rows(blk, carry):
        at = pl.ds(pl.multiple_of(blk * 16, 16), 16)
        c = col2[at, :]
        mg = c[:, 30:31] * pbuf[0, at, :] - c[:, 31:32] * mixed[at, :]
        g = [gs[j, at, :].astype(F32) for j in range(4)]
        for i in range(4):
            o = 32 * i + 24
            v = acc[i, at, :] + c[:, o : o + 1] * mg - c[:, o + 1 : o + 2] * xs[i, at, :].astype(F32)
            for j in range(4):
                v = v + c[:, o + 2 + j : o + 3 + j] * g[j]
            so_v[i, at, :] = v.astype(BF16)
        return carry

    ag_forward(4)
    lax.fori_loop(0, T // 16, out_rows, 0)
    so_out = pltpu.make_async_copy(so_v, so_h, out_sem.at[1])
    so_out.start()

    red_forward(1)
    pair_start(2)

    def sm_x(k):
        return rcopy(sx.at[x], sx.at[x], sm_ss.at[k], sm_rs.at[k], xdev(k))

    def sm_x_in(k):
        at = sx.at[lax.rem(x - k + NX, NX)]
        return rcopy(at, at, sm_ss.at[k], sm_rs.at[k], xdev(k))

    def sm_y(k):
        return rcopy(sy.at[y], sy.at[y], sm_ss.at[3 + k], sm_rs.at[3 + k], ydev(k))

    def sm_y_in(k):
        at = sy.at[lax.rem(y - k + NY, NY)]
        return rcopy(at, at, sm_ss.at[3 + k], sm_rs.at[3 + k], ydev(k))

    sm_core.wait_recv()
    sx[x] = sb[...] + sc[...]
    for k in (1, 2, 3):
        sm_x(k).start()

    ag_in(RIGHT, 4, 0).wait_recv()
    ag_in(LEFT, 4, 1).wait_recv()
    pair_start(3)
    red_forward(2)
    red_forward(3)

    for k in (1, 2, 3):
        sm_x_in(k).wait_recv()
    sy[y] = sx[0] + sx[1] + sx[2] + sx[3]
    for k in (1, 2, 3):
        sm_y(k).start()

    for m in range(4):
        pair_finish(m)

    red_start(4, lambda r: xa[lax.rem(y + r, NY)])
    for k in (1, 2, 3):
        sm_y_in(k).wait_recv()
    small = sy[0] + sy[1] + sy[2] + sy[3]
    cw_o[...] = small[0:6]
    gain_o[...] = small[6:7]
    lane = lax.broadcasted_iota(jnp.int32, (8, 128), 1)
    st8 = jnp.zeros((8, 128), F32)
    for i in range(4):
        st8 = jnp.where(lane == i, small[8:16, i * 128 : i * 128 + 128], st8)
    st_o[...] = st8
    red_forward(4)
    top, low = red_finish(4, xa[y])
    wo_v[:HB] = top
    wo_v[HB:] = low
    wo_out = pltpu.make_async_copy(wo_v, wo_h, out_sem.at[2])
    wo_out.start()

    for way in (RIGHT, LEFT):
        for step in range(4):
            for half in range(2):
                if step or half == way:
                    rs_copy(way, step, half).wait_send()
        for step in range(1, 5):
            for kk in range(2):
                if step < 4 or kk == way:
                    ag_copy(way, step, kk).wait_send()
        for e in range(5):
            for part in range(3):
                red_copy(e, way, part).wait_send()
    for k in range(1, NZ):
        sync_out(k).wait_send()
        sync_back(k).wait_send()
        h_out(k).wait_send()
    q_swap.wait_send()
    for kk in range(2):
        n_swap(kk).wait_send()
    sm_core.wait_send()
    for k in (1, 2, 3):
        sm_x(k).wait_send()
        sm_y(k).wait_send()
    bo_out.wait()
    so_out.wait()
    wo_out.wait()


def local(streams, stream_grads, branch_out, query_grads, query_weight, norm_gain, coef_weight, static_coef):
    any_spec = pl.BlockSpec(memory_space=pl.ANY)
    vmem = pl.BlockSpec(memory_space=pltpu.VMEM)
    smem = pl.BlockSpec(memory_space=pltpu.SMEM)
    dma = pltpu.SemaphoreType.DMA
    outs = pl.pallas_call(
        kernel,
        out_shape=(
            jax.ShapeDtypeStruct((4, T, F), BF16),
            jax.ShapeDtypeStruct((T, F), BF16),
            jax.ShapeDtypeStruct((RB, F), F32),
            jax.ShapeDtypeStruct((1, F), F32),
            jax.ShapeDtypeStruct((6, F), F32),
            jax.ShapeDtypeStruct((8, 128), F32),
        ),
        in_specs=[any_spec] * 5 + [vmem, vmem, smem],
        out_specs=(any_spec, any_spec, any_spec, vmem, vmem, vmem),
        scratch_shapes=[
            pltpu.VMEM((5, T, F), BF16),
            pltpu.VMEM((4, T, F), BF16),
            pltpu.VMEM((2, T, F), BF16),
            pltpu.VMEM((NZ, F, F), BF16),
            pltpu.VMEM((NZ, T, F), F32),
            pltpu.VMEM((2, 4, 2, T // 2, F), BF16),
            pltpu.VMEM((2, 4, 2, T // 2, F), BF16),
            pltpu.VMEM((NZ, 8, T), F32),
            pltpu.VMEM((NZ, 8, T), F32),
            pltpu.VMEM((NZ, 8, T), F32),
            pltpu.VMEM((NZ, 8, T), F32),
            pltpu.VMEM((T, F), F32),
            pltpu.VMEM((F, T), BF16),
            pltpu.VMEM((NZ, 2, 2, RB, T), BF16),
            pltpu.VMEM((T, 128), F32),
            pltpu.VMEM((T, 128), F32),
            pltpu.VMEM((4, 128, F), BF16),
            pltpu.VMEM((5, 2, 3, HB, F), BF16),
            pltpu.VMEM((5, 2, 3, HB, F), BF16),
            pltpu.VMEM((5, 2, HB, F), F32),
            pltpu.VMEM((NY, RB, F), F32),
            pltpu.VMEM((RB, F), F32),
            pltpu.VMEM((4, T, F), BF16),
            pltpu.VMEM((T, F), BF16),
            pltpu.VMEM((4, T, F), F32),
            pltpu.VMEM((16, F), F32),
            pltpu.VMEM((16, F), F32),
            pltpu.VMEM((NX, 16, F), F32),
            pltpu.VMEM((NY, 16, F), F32),
            dma((4,)),
            dma((NZ,)),
            dma((3,)),
            dma((2, 4, 2)),
            dma((2, 4, 2)),
            dma((2, 5, 2)),
            dma((2, 5, 2)),
            dma((3, NZ)),
            dma((3, NZ)),
            dma((3,)),
            dma((3,)),
            dma((5, 2, 3)),
            dma((5, 2, 3)),
            dma((7,)),
            dma((7,)),
        ],
        compiler_params=pltpu.CompilerParams(
            collective_id=0, has_side_effects=True, vmem_limit_bytes=56 * 1024 * 1024
        ),
        cost_estimate=pl.CostEstimate(flops=8_000_000_000, bytes_accessed=13_000_000, transcendentals=10000),
    )(
        streams,
        stream_grads,
        branch_out,
        query_grads,
        query_weight,
        norm_gain.reshape(1, F),
        coef_weight.T,
        static_coef,
    )
    so, bo, wo, gain, cwg, stat = outs
    return so, bo, wo, gain.reshape(F), cwg.T, stat[0:6, 0:4].T


def solution(mesh):
    in_specs = (
        P(None, "dp", "tensor"),
        P(None, "dp", "tensor"),
        P("dp", "tensor"),
        P("dp", "tensor"),
        P(None, "tensor"),
        P("tensor"),
        P("tensor", None),
        P(),
    )
    out_specs = (
        P(None, "dp", "tensor"),
        P("dp", "tensor"),
        P("dp", "tensor"),
        P("tensor"),
        P("tensor", None),
        P(),
    )
    return jax.shard_map(local, mesh=mesh, in_specs=in_specs, out_specs=out_specs, check_vma=False)
```

time: 339 us -> 105 us (0.31)
  the two profiles are of different devices: /device:TPU:1 before, /device:TPU:8 now
where the time goes in v1:
time: 105 us
  Pallas kernels  95.8 us (91%)
  local copies, waits for them, and re-layouts  7.26 us (7%)
  other arithmetic  1.29 us (1%)
    pallas_call x1, Pallas kernels, local(): pl.pallas_call(kernel, out_shape=(jax.ShapeDtypeStruct((4, T, F), BF16),...  95.8 us
    unnamed x11, local copies, waits for them, and re-layouts  5.31 us

profile of v1, /device:TPU:8, one launch (start us, length us, event | category | flops | bytes accessed | tf_op | source)
XLA Modules:
  0.0 105.0 jit_solution(4586905973519674871)
XLA Ops:
  0.6 1.3 %reshape.18.gain = f32[1,640]{1,0:T(1,128)} reshape(f32[640]{0:T(1024)} %param.13) | data formatting | bytes 5120 | tf_op jit(solution)/shard_map/reshape | solution.py:656
  1.9 95.8 %shard_map.127 = (bf16[4,256,640]{2,1,0:T(8,128)(2,1)}, bf16[256,640]{1,0:T(8,128)(2,1)}, f32[160,640]{1,0:T(8,128)}, f32[1,640]{1,0:T(1,128)}, f32[6,640]{1,0:T(8,128)}, /*index=5*/f32[8,128]{1,0:T(8,128)}) custom-call(bf16[4,256,640]{2,1,0:T(8,128)(2,1)} %s_h.1, bf16[4,256,640]{2,1,0:T(8,128)(2,1)} %g_h.1, bf16[256,640]{1,0:T(8,128)(2,1)} %b_h.1, ...), custom_call_target="tpu_custom_call" | custom-call | flops 8000000000 | bytes 13000000 | tf_op jit(solution)/shard_map/pallas_call | solution.py:588
  97.7 1.3 %reduce = f32[640]{0:T(1024)} reduce(f32[1,640]{1,0:T(1,128)} %get-tuple-element.15, f32[]{:T(128)} %constant), dimensions={0}, to_apply=%get-tuple-element.15.reduce_sub_computation | reduce | bytes 5124 | tf_op jit(solution)/shard_map/pallas_call | solution.py:588
  99.0 0.7 slice_bitcast_fusion
  99.7 0.7 copy.14
  100.4 0.0 copy-start.1
  100.4 0.0 copy-start
  100.4 2.6 %copy.19 = bf16[4,256,640]{2,1,0:T(8,128)(2,1)} copy(bf16[4,256,640]{2,1,0:T(8,128)(2,1)} %get-tuple-element.30) | data formatting | bytes 2621440
  102.9 0.0 copy-done.1
  102.9 0.0 copy-start.2
  102.9 0.7 copy.20
  103.7 0.0 copy-done
  103.7 0.8 copy.21
  104.4 0.0 copy-done.2
  104.4 0.6 copy.22
Async XLA Ops:
  100.4 2.6 %copy-start.1 = (bf16[256,640]{1,0:T(8,128)(2,1)S(1)}, bf16[256,640]{1,0:T(8,128)(2,1)}, u32[]{:S(2)}) copy-start(bf16[256,640]{1,0:T(8,128)(2,1)} %get-tuple-element.31) | copy-start | bytes 983044
  100.4 3.3 %copy-start = (f32[160,640]{1,0:T(8,128)S(1)}, f32[160,640]{1,0:T(8,128)}, u32[]{:S(2)}) copy-start(f32[160,640]{1,0:T(8,128)} %get-tuple-element.32) | copy-start | bytes 1228804
  102.9 1.5 %copy-start.2 = (f32[6,640]{1,0:T(8,128)S(1)}, f32[6,640]{1,0:T(8,128)}, u32[]{:S(2)}) copy-start(f32[6,640]{1,0:T(8,128)} %get-tuple-element.16) | copy-start | bytes 46084

commit v2 on v1

--- a/solution.py
+++ b/solution.py
@@ -42,8 +42,8 @@
     so_h, bo_h, wo_h, gain_o, cw_o, st_o,
     xs, gs, qq, wbuf,
     pbuf, rs_send, rs_recv,
-    cl, r1, cfull, hbuf,
-    mixed, nts, nbuf, col1, col2, cwx,
+    cl, r1, cfull, crit, crit_r, crit_f, hbuf,
+    mixed, nts, nbuf, col1, colb, col2, cwx,
     xsend, xrecv, keep, xa, wo_v,
     so_v, bo_v, acc, sb, sc, sx, sy,
     in_sem, win_sem, out_sem,
@@ -71,6 +71,8 @@
             src_ref=src, dst_ref=dst, send_sem=ss, recv_sem=rs, device_id=dev, device_id_type=MESH
         )
 
+    gain_row = jnp.concatenate([gain[i : i + 1, :] for i in range(F // 128)], axis=1)
+
     q_in = pltpu.make_async_copy(q_h, qq.at[core], in_sem.at[0])
     s_in = pltpu.make_async_copy(s_h, xs.at[0:4], in_sem.at[1])
     g_in = pltpu.make_async_copy(g_h, gs, in_sem.at[2])
@@ -82,12 +84,13 @@
             w_h.at[pl.ds(pl.multiple_of(blk * F, F), F)], wbuf.at[k], win_sem.at[k]
         )
 
+    s_in.start()
     q_in.start()
-    w_in(4).start()
-    s_in.start()
+    for k in (4, 3, 5):
+        w_in(k).start()
     g_in.start()
     b_in.start()
-    for k in (3, 5, 2, 6, 1, 7, 0):
+    for k in (2, 6, 1, 7, 0):
         w_in(k).start()
 
     barrier = pltpu.get_barrier_semaphore()
@@ -125,21 +128,7 @@
         rs_send[way, step, half] = (v + rs_recv[way, step - 1, half].astype(F32)).astype(BF16)
         rs_copy(way, step, half).start()
 
-    q_in.wait()
-    rs_partial(4)
-    pl.semaphore_wait(barrier, len(peers))
-    rs_raw(RIGHT, 0, 0)
-    rs_raw(LEFT, 0, 1)
-    q_swap = rcopy(qq.at[core], qq.at[core], core_ss.at[0], core_rs.at[0], cdev)
-    q_swap.start()
-    rs_partial(3)
-    rs_raw(RIGHT, 1, 1)
-    rs_partial(5)
-    rs_raw(LEFT, 1, 0)
-
     s_in.wait()
-    g_in.wait()
-    b_in.wait()
     cw8 = jnp.concatenate([cw[...].astype(F32), jnp.zeros((10, F), F32)], axis=0).astype(BF16)
     rows_i = lax.broadcasted_iota(jnp.int32, (128, 128), 0)
     cols_i = lax.broadcasted_iota(jnp.int32, (128, 128), 1)
@@ -148,7 +137,26 @@
     def diag(block):
         return jnp.sum(jnp.where(eye, block, 0.0), axis=0, keepdims=True)
 
-    def gram(blk, carry):
+    def gram_s(blk, carry):
+        at = pl.ds(pl.multiple_of(blk * 128, 128), 128)
+        s_blk = xs[0:4, at, :].reshape(4 * 128, F)
+        ss = dot_nt(s_blk, s_blk)
+        gr = {
+            (i, j): diag(ss[i * 128 : i * 128 + 128, j * 128 : j * 128 + 128])
+            for i in range(4)
+            for j in range(i, 4)
+        }
+        proj = dot_nt(cw8, s_blk)
+        for i in range(4):
+            cl[i, 0:7, at] = jnp.concatenate([proj[0:6, i * 128 : i * 128 + 128], gr[i, i]], axis=0)
+        off = [gr[0, 1], gr[0, 2], gr[0, 3], gr[1, 2], gr[1, 3], gr[2, 3]]
+        first = [proj[1:2, i * 128 : i * 128 + 128] for i in range(4)]
+        first += [gr[i, i] for i in range(4)] + off + [jnp.zeros((1, 128), F32)] * 2
+        for p in range(NZ):
+            crit[p, :, at] = jnp.concatenate(first[2 * p : 2 * p + 2], axis=0)
+        return carry
+
+    def gram_g(blk, carry):
         at = pl.ds(pl.multiple_of(blk * 128, 128), 128)
         sb_blk = xs[:, at, :].reshape(5 * 128, F)
         g_blk = gs[:, at, :].reshape(4 * 128, F)
@@ -156,30 +164,17 @@
         route = [
             [diag(sg[i * 128 : i * 128 + 128, j * 128 : j * 128 + 128]) for j in range(4)] for i in range(5)
         ]
-        s_blk = sb_blk[: 4 * 128]
-        ss = dot_nt(s_blk, s_blk)
-        gr = {
-            (i, j): diag(ss[i * 128 : i * 128 + 128, j * 128 : j * 128 + 128])
-            for i in range(4)
-            for j in range(i, 4)
-        }
-        proj = dot_nt(cw8, s_blk)
-        zero = jnp.zeros((1, 128), F32)
         for i in range(4):
-            cl[i, :, at] = jnp.concatenate(
-                [proj[0:6, i * 128 : i * 128 + 128], gr[i, i], route[4][i]], axis=0
-            )
+            cl[i, 7:8, at] = route[4][i]
         for half in range(2):
             cl[4 + half, :, at] = jnp.concatenate(
                 [route[2 * half + i][j] for i in range(2) for j in range(4)], axis=0
             )
-        cl[6, :, at] = jnp.concatenate(
-            [gr[0, 1], gr[0, 2], gr[0, 3], gr[1, 2], gr[1, 3], gr[2, 3], zero, zero], axis=0
-        )
-        cl[7, :, at] = jnp.zeros((8, 128), F32)
         return carry
 
-    lax.fori_loop(0, 2, gram, 0)
+    lax.fori_loop(0, 2, gram_s, 0)
+    for p in (6, 7):
+        cl[p] = jnp.zeros((8, T), F32)
 
     def sync_out(k):
         return rcopy(
@@ -193,27 +188,42 @@
         at = cfull.at[lax.rem(z - k + NZ, NZ)]
         return rcopy(at, at, sync_ss.at[1, k], sync_rs.at[1, k], zdev(k))
 
-    for k in range(1, NZ):
-        sync_out(k).start()
-
+    def crit_out(k):
+        return rcopy(
+            crit.at[lax.rem(z + k, NZ)], crit_r.at[k], sync_ss.at[3, k], sync_rs.at[3, k], zdev(k)
+        )
+
+    def crit_back(k):
+        return rcopy(crit_f.at[z], crit_f.at[z], sync_ss.at[4, k], sync_rs.at[4, k], zdev(k))
+
+    def crit_back_in(k):
+        at = crit_f.at[lax.rem(z - k + NZ, NZ)]
+        return rcopy(at, at, sync_ss.at[4, k], sync_rs.at[4, k], zdev(k))
+
+    q_in.wait()
+    for k in (4, 3, 5):
+        rs_partial(k)
+
+    pl.semaphore_wait(barrier, len(peers))
+    for k in range(1, NZ):
+        crit_out(k).start()
+    rs_raw(RIGHT, 0, 0)
+    rs_raw(LEFT, 0, 1)
+    q_swap = rcopy(qq.at[core], qq.at[core], core_ss.at[0], core_rs.at[0], cdev)
+    q_swap.start()
     rs_partial(2)
-    rs_partial(6)
-    rs_add(RIGHT, 1, 0)
-    rs_add(LEFT, 1, 1)
-
-    total = cl[z]
-    for k in range(1, NZ):
-        sync_out(k).wait_recv()
-        total = total + r1[k]
-    cfull[z] = total
-    for k in range(1, NZ):
-        sync_back(k).start()
-
-    rs_add(RIGHT, 2, 1)
-    rs_add(LEFT, 2, 0)
-    rs_partial(1)
-    rs_partial(7)
-    rs_partial(0)
+    first = crit[z]
+    for k in range(1, NZ):
+        crit_out(k).wait_recv()
+        first = first + crit_r[k]
+    crit_f[z] = first
+    for k in range(1, NZ):
+        crit_back(k).start()
+    rs_raw(RIGHT, 1, 1)
+    rs_raw(LEFT, 1, 0)
+    g_in.wait()
+    b_in.wait()
+    lax.fori_loop(0, 2, gram_g, 0)
 
     cw_f = cw8[0:8].astype(F32)
     for i in range(4):
@@ -223,17 +233,20 @@
         parts = parts + [jnp.zeros((128 - i * 32 - 24, F), F32)]
         cwx[i] = jnp.concatenate(parts, axis=0).astype(BF16)
 
-    for k in range(1, NZ):
-        sync_back_in(k).wait_recv()
-
     row8 = lax.broadcasted_iota(jnp.int32, (8, T), 0)
 
     def coefficients():
         proj, inv, sq, cf = [], [], [], []
+        at = {(0, 1): 8, (0, 2): 9, (0, 3): 10, (1, 2): 11, (1, 3): 12, (2, 3): 13}
+
+        def g_of(i, j):
+            r = 4 + i if i == j else at[min(i, j), max(i, j)]
+            return crit_f[r // 2, r % 2 : r % 2 + 1]
+
         for i in range(4):
             piece = cfull[i]
             p8 = jnp.where(row8 < 6, piece, 0.0)
-            iv = lax.rsqrt(piece[6:7] / D + EPS)
+            iv = lax.rsqrt(g_of(i, i) / D + EPS)
             th = jnp.tanh(iv * p8)
             stc = jnp.zeros((8, T), F32)
             for c in range(6):
@@ -242,38 +255,40 @@
             inv.append(iv)
             sq.append(th)
             cf.append(stc + th)
-        off = cfull[6]
-        at = {(0, 1): 0, (0, 2): 1, (0, 3): 2, (1, 2): 3, (1, 3): 4, (2, 3): 5}
-
-        def g_of(i, j):
-            if i == j:
-                return cfull[i][6:7]
-            r = at[min(i, j), max(i, j)]
-            return off[r : r + 1]
-
         wid = [cf[i][1:2] for i in range(4)]
         gw = [sum(g_of(i, j) * wid[j] for j in range(4)) for i in range(4)]
         mixed_sq = sum(wid[i] * gw[i] for i in range(4))
         mix_inv = lax.rsqrt(mixed_sq / D + EPS)
         return proj, inv, sq, cf, wid, gw, mix_inv
 
-    _, _, _, cf, _, _, mix_inv = coefficients()
-    rows = jnp.concatenate(cf + [jnp.broadcast_to(mix_inv, (8, T)), jnp.zeros((88, T), F32)], axis=0)
-    col1[...] = rows.T
+    for k in range(1, NZ):
+        crit_back_in(k).wait_recv()
+
+    def mix_coefficients():
+        low = jnp.concatenate([crit_f[p] for p in range(4)], axis=0)
+        high = jnp.concatenate([crit_f[p] for p in range(4, 7)], axis=0)
+        wid = [
+            st[i, 1] + jnp.tanh(lax.rsqrt(low[4 + i : 5 + i] / D + EPS) * low[i : i + 1]) for i in range(4)
+        ]
+        at = {(0, 1): 0, (0, 2): 1, (0, 3): 2, (1, 2): 3, (1, 3): 4, (2, 3): 5}
+        mixed_sq = sum(wid[i] * wid[i] * low[4 + i : 5 + i] for i in range(4))
+        mixed_sq = mixed_sq + 2.0 * sum(wid[i] * wid[j] * high[r : r + 1] for (i, j), r in at.items())
+        return wid, lax.rsqrt(mixed_sq / D + EPS)
+
+    wid, mix_inv = mix_coefficients()
+    col1[...] = jnp.concatenate(wid + [mix_inv, jnp.zeros((123, T), F32)], axis=0).T
 
     def mix(blk, carry):
         at = pl.ds(pl.multiple_of(blk * 32, 32), 32)
         c = col1[at, :]
-        m = c[:, 1:2] * xs[0, at, :].astype(F32)
+        m = c[:, 0:1] * xs[0, at, :].astype(F32)
         for i in range(1, 4):
-            m = m + c[:, 8 * i + 1 : 8 * i + 2] * xs[i, at, :].astype(F32)
+            m = m + c[:, i : i + 1] * xs[i, at, :].astype(F32)
         mixed[at, :] = m
-        acc[0, at, :] = m * c[:, 32:33] * gain[...]
+        acc[0, at, :] = m * c[:, 4:5] * gain_row
         return carry
 
     lax.fori_loop(0, T // 32, mix, 0)
-    for k in range(4):
-        pass
     for lane in range(F // 128):
         tr = acc[0, :, lane * 128 : lane * 128 + 128].T.astype(BF16)
         nts[lane * 128 : lane * 128 + 128, :] = tr
@@ -301,8 +316,8 @@
     for kk in range(2):
         nbuf[z, kk, core] = nts[pl.ds(pl.multiple_of((2 * kk + core) * RB, 32), RB), :]
 
-    rs_add(RIGHT, 2, 0)
-    rs_add(LEFT, 2, 1)
+    rs_add(RIGHT, 1, 0)
+    rs_add(LEFT, 1, 1)
 
     def ag_copy(way, step, kk):
         blk = lax.rem(z - step + 1 + NZ, NZ) if way == RIGHT else lax.rem(z + step - 1, NZ)
@@ -314,22 +329,24 @@
         at = nbuf.at[blk, kk]
         return rcopy(at, at, ag_ss.at[way, step, kk], ag_rs.at[way, step, kk], zdev(1 if way == RIGHT else -1))
 
-    for kk in range(2):
-        n_swap_in(kk).wait_recv()
-        ag_copy(RIGHT, 1, kk).start()
-        ag_copy(LEFT, 1, kk).start()
+    n_swap_in(0).wait_recv()
+    ag_copy(RIGHT, 1, 0).start()
+    n_swap_in(1).wait_recv()
+    ag_copy(LEFT, 1, 1).start()
+    ag_copy(RIGHT, 1, 1).start()
+    ag_copy(LEFT, 1, 0).start()
 
     def ag_forward(step):
-        for kk in range(2):
+        for first in range(2):
             for way in (RIGHT, LEFT):
-                ag_in(way, step - 1, kk).wait_recv()
+                kk = first ^ way
                 if step < 4 or kk == way:
+                    ag_in(way, step - 1, kk).wait_recv()
                     ag_copy(way, step, kk).start()
 
     par = lax.rem(z, 2)
     z0 = z - par
     q_swap_in = rcopy(qq.at[1 - core], qq.at[1 - core], core_ss.at[0], core_rs.at[0], cdev)
-    q_swap_in.wait_recv()
 
     def pair_base(m):
         if m == 0:
@@ -391,33 +408,56 @@
 
     def branch(blk, carry):
         at = pl.ds(pl.multiple_of(blk * 32, 32), 32)
-        c = col1[at, :]
+        c = colb[at, :]
         v = c[:, 0:1] * gs[0, at, :].astype(F32)
         for j in range(1, 4):
-            v = v + c[:, 8 * j : 8 * j + 1] * gs[j, at, :].astype(F32)
+            v = v + c[:, j : j + 1] * gs[j, at, :].astype(F32)
         bo_v[at, :] = v.astype(BF16)
         return carry
 
-    rs_add(RIGHT, 3, 1)
-    rs_add(LEFT, 3, 0)
-    lax.fori_loop(0, T // 32, branch, 0)
-    bo_out = pltpu.make_async_copy(bo_v, bo_h, out_sem.at[0])
-    bo_out.start()
-    rs_add(RIGHT, 3, 0)
-    rs_add(LEFT, 3, 1)
+    rs_partial(6)
+    rs_add(RIGHT, 2, 1)
+    rs_add(LEFT, 2, 0)
+    for k in (1, 7, 0):
+        rs_partial(k)
+    q_swap_in.wait_recv()
 
     ag_forward(2)
+    rs_add(RIGHT, 2, 0)
+    rs_add(LEFT, 2, 1)
     pair_start(0)
 
-    for way in (RIGHT, LEFT):
-        for half in range(2):
-            rs_copy(way, 3, half).wait_recv()
-
-    def norm(blk, gain_sum):
-        at = pl.ds(pl.multiple_of(blk * 128, 128), 128)
+    red_forward(0)
+
+    ag_forward(3)
+    pair_start(1)
+    red_forward(1)
+
+    ag_forward(4)
+    for half in (1, 0):
+        for way in (RIGHT, LEFT):
+            rs_add(way, 3, half)
+    for k in range(1, NZ):
+        sync_out(k).start()
+    ag_in(RIGHT, 3, 1).wait_recv()
+    ag_in(LEFT, 3, 0).wait_recv()
+    pair_start(2)
+    pair_finish(0)
+    red_forward(2)
+
+    ag_in(RIGHT, 4, 0).wait_recv()
+    ag_in(LEFT, 4, 1).wait_recv()
+    pair_start(3)
+    pair_finish(1)
+    pair_finish(2)
+
+    def norm(blk):
+        at = slice(blk * 128, blk * 128 + 128)
+        for way in (RIGHT, LEFT):
+            rs_copy(way, 3, blk).wait_recv()
         ng = pbuf[0, at, :] + rs_recv[RIGHT, 3, blk].astype(F32) + rs_recv[LEFT, 3, blk].astype(F32)
-        gain_sum = gain_sum + jnp.sum(ng * (mixed[at, :] * col1[at, 32:33]), axis=0, keepdims=True)
-        scaled = ng * gain[...]
+        gain_sum = jnp.sum(ng * (mixed[at, :] * col1[at, 4:5]), axis=0, keepdims=True)
+        scaled = ng * gain_row
         pbuf[0, at, :] = scaled
         hi, mid, lo = split3(scaled)
         parts = jnp.concatenate([hi, mid, lo], axis=0).astype(BF16)
@@ -426,10 +466,16 @@
         for i in range(4):
             p = prod[i * 128 : i * 128 + 128]
             h.append(diag(p[:, 0:128] + p[:, 128:256] + p[:, 256:384]))
-        hbuf[z, :, at] = jnp.concatenate(h + [jnp.zeros((4, 128), F32)], axis=0)
+        hbuf[z, 4 * blk : 4 * blk + 4, :] = jnp.concatenate(h, axis=0)
         return gain_sum
 
-    gain_part = lax.fori_loop(0, T // 128, norm, jnp.zeros((1, F), F32))
+    gain_part = norm(1)
+    total = cl[z]
+    for k in range(1, NZ):
+        sync_out(k).wait_recv()
+        total = total + r1[k]
+    cfull[z] = total
+    gain_part = gain_part + norm(0)
 
     def h_out(k):
         return rcopy(hbuf.at[z], hbuf.at[z], sync_ss.at[2, k], sync_rs.at[2, k], zdev(k))
@@ -440,21 +486,29 @@
 
     for k in range(1, NZ):
         h_out(k).start()
-
-    red_forward(0)
-    ag_forward(3)
-    pair_start(1)
+    for k in range(1, NZ):
+        sync_back(k).start()
+
+    red_forward(3)
+    pair_finish(3)
+    red_start(4, lambda r: xa[lax.rem(y + r, NY)])
 
     for k in range(1, NZ):
         h_in(k).wait_recv()
+    for k in range(1, NZ):
+        sync_back_in(k).wait_recv()
 
     proj, inv, sq, cf, wid, gw, mix_inv = coefficients()
     h8 = hbuf[0]
     for k in range(1, NZ):
         h8 = h8 + hbuf[k]
+    h8 = jnp.concatenate([h8[0:4], h8[4:8]], axis=1)
     inner = sum(wid[i] * h8[i : i + 1] for i in range(4))
     kfac = mix_inv * mix_inv * mix_inv * inner / D
-    rows, left, stat = [], [], []
+    rows, left = [], []
+    sub8 = lax.broadcasted_iota(jnp.int32, (8, 128), 0)
+    lane8 = lax.broadcasted_iota(jnp.int32, (8, 128), 1)
+    stat = jnp.zeros((1, 128), F32)
     for i in range(4):
         mix_grad = mix_inv * h8[i : i + 1] - kfac * gw[i]
         route = cfull[4 + i // 2][4 * (i % 2) : 4 * (i % 2) + 4]
@@ -465,12 +519,13 @@
         hi, mid, lo = split3(pg)
         left.append(jnp.concatenate([hi, mid, lo], axis=0))
         rows += [hi, mid, lo, wid[i], scale, cf[i][2:6], mix_inv, kfac]
-        stat.append(jnp.broadcast_to(jnp.sum(cg, axis=1, keepdims=True), (8, 128)))
+        sums = jnp.broadcast_to(jnp.sum(cg, axis=1, keepdims=True), (8, 128))
+        stat = stat + jnp.sum(jnp.where(lane8 == sub8 + 8 * i, sums, 0.0), axis=0, keepdims=True)
     col2[...] = jnp.concatenate(rows, axis=0).T
     cpart = dot_nn(jnp.concatenate(left, axis=1).astype(BF16), xs[0:4].reshape(4 * T, F))
     cpart = cpart[0:8] + cpart[8:16] + cpart[16:24]
-    sb[0:8, :] = jnp.concatenate([cpart[0:6], gain_part, jnp.zeros((1, F), F32)], axis=0)
-    sb[8:16, :] = jnp.concatenate(stat + [jnp.zeros((8, 128), F32)], axis=1)
+    last = jnp.concatenate([stat, jnp.zeros((1, F - 128), F32)], axis=1)
+    sb[...] = jnp.concatenate([cpart[0:6], gain_part, last], axis=0)
 
     sm_core = rcopy(sb, sc, sm_ss.at[0], sm_rs.at[0], cdev)
     sm_core.start()
@@ -492,14 +547,6 @@
             so_v[i, at, :] = v.astype(BF16)
         return carry
 
-    ag_forward(4)
-    lax.fori_loop(0, T // 16, out_rows, 0)
-    so_out = pltpu.make_async_copy(so_v, so_h, out_sem.at[1])
-    so_out.start()
-
-    red_forward(1)
-    pair_start(2)
-
     def sm_x(k):
         return rcopy(sx.at[x], sx.at[x], sm_ss.at[k], sm_rs.at[k], xdev(k))
 
@@ -518,39 +565,34 @@
     sx[x] = sb[...] + sc[...]
     for k in (1, 2, 3):
         sm_x(k).start()
-
-    ag_in(RIGHT, 4, 0).wait_recv()
-    ag_in(LEFT, 4, 1).wait_recv()
-    pair_start(3)
-    red_forward(2)
-    red_forward(3)
-
+    red_forward(4)
+
+    lax.fori_loop(0, T // 32, out_rows, 0)
     for k in (1, 2, 3):
         sm_x_in(k).wait_recv()
     sy[y] = sx[0] + sx[1] + sx[2] + sx[3]
     for k in (1, 2, 3):
         sm_y(k).start()
-
-    for m in range(4):
-        pair_finish(m)
-
-    red_start(4, lambda r: xa[lax.rem(y + r, NY)])
-    for k in (1, 2, 3):
-        sm_y_in(k).wait_recv()
-    small = sy[0] + sy[1] + sy[2] + sy[3]
-    cw_o[...] = small[0:6]
-    gain_o[...] = small[6:7]
-    lane = lax.broadcasted_iota(jnp.int32, (8, 128), 1)
-    st8 = jnp.zeros((8, 128), F32)
-    for i in range(4):
-        st8 = jnp.where(lane == i, small[8:16, i * 128 : i * 128 + 128], st8)
-    st_o[...] = st8
-    red_forward(4)
+    lax.fori_loop(T // 32, T // 16, out_rows, 0)
+    colb[...] = jnp.concatenate([cf[j][0:1] for j in range(4)] + [jnp.zeros((124, T), F32)], axis=0).T
+    lax.fori_loop(0, T // 32, branch, 0)
+    bo_out = pltpu.make_async_copy(bo_v, bo_h, out_sem.at[0])
+    bo_out.start()
+    so_out = pltpu.make_async_copy(so_v, so_h, out_sem.at[1])
+    so_out.start()
+
     top, low = red_finish(4, xa[y])
     wo_v[:HB] = top
     wo_v[HB:] = low
     wo_out = pltpu.make_async_copy(wo_v, wo_h, out_sem.at[2])
     wo_out.start()
+
+    for k in (1, 2, 3):
+        sm_y_in(k).wait_recv()
+    small = sy[0] + sy[1] + sy[2] + sy[3]
+    cw_o[...] = small[0:6]
+    gain_o[...] = jnp.concatenate([small[6:7, i * 128 : i * 128 + 128] for i in range(F // 128)], axis=0)
+    st_o[...] = jnp.concatenate([small[7:8, 8 * i : 8 * i + 6] for i in range(4)], axis=0)
 
     for way in (RIGHT, LEFT):
         for step in range(4):
@@ -567,6 +609,8 @@
     for k in range(1, NZ):
         sync_out(k).wait_send()
         sync_back(k).wait_send()
+        crit_out(k).wait_send()
+        crit_back(k).wait_send()
         h_out(k).wait_send()
     q_swap.wait_send()
     for kk in range(2):
@@ -580,6 +624,28 @@
     wo_out.wait()
 
 
+def copy_kernel(*refs):
+    src, dst, held, sem = refs[:6], refs[6:12], refs[12:15], refs[15]
+    pieces = [(0, (i, pl.ds(h, T // 2))) for i in range(4) for h in (0, T // 2)]
+    pieces += [(1, (pl.ds(h, T // 2),)) for h in (0, T // 2)]
+    pieces += [(2, (pl.ds(h, HB),)) for h in (0, HB)]
+    loads = [
+        pltpu.make_async_copy(src[i].at[at], held[i].at[at], sem.at[0, n]) for n, (i, at) in enumerate(pieces)
+    ]
+    stores = [
+        pltpu.make_async_copy(held[i].at[at], dst[i].at[at], sem.at[1, n]) for n, (i, at) in enumerate(pieces)
+    ]
+    for c in loads:
+        c.start()
+    for i in range(3, 6):
+        dst[i][...] = src[i][...]
+    for load, store in zip(loads, stores):
+        load.wait()
+        store.start()
+    for c in stores:
+        c.wait()
+
+
 def local(streams, stream_grads, branch_out, query_grads, query_weight, norm_gain, coef_weight, static_coef):
     any_spec = pl.BlockSpec(memory_space=pl.ANY)
     vmem = pl.BlockSpec(memory_space=pltpu.VMEM)
@@ -591,9 +657,9 @@
             jax.ShapeDtypeStruct((4, T, F), BF16),
             jax.ShapeDtypeStruct((T, F), BF16),
             jax.ShapeDtypeStruct((RB, F), F32),
-            jax.ShapeDtypeStruct((1, F), F32),
+            jax.ShapeDtypeStruct((F // 128, 128), F32),
             jax.ShapeDtypeStruct((6, F), F32),
-            jax.ShapeDtypeStruct((8, 128), F32),
+            jax.ShapeDtypeStruct((4, 6), F32),
         ),
         in_specs=[any_spec] * 5 + [vmem, vmem, smem],
         out_specs=(any_spec, any_spec, any_spec, vmem, vmem, vmem),
@@ -608,10 +674,14 @@
             pltpu.VMEM((NZ, 8, T), F32),
             pltpu.VMEM((NZ, 8, T), F32),
             pltpu.VMEM((NZ, 8, T), F32),
-            pltpu.VMEM((NZ, 8, T), F32),
+            pltpu.VMEM((NZ, 2, T), F32),
+            pltpu.VMEM((NZ, 2, T), F32),
+            pltpu.VMEM((NZ, 2, T), F32),
+            pltpu.VMEM((NZ, 8, 128), F32),
             pltpu.VMEM((T, F), F32),
             pltpu.VMEM((F, T), BF16),
             pltpu.VMEM((NZ, 2, 2, RB, T), BF16),
+            pltpu.VMEM((T, 128), F32),
             pltpu.VMEM((T, 128), F32),
             pltpu.VMEM((T, 128), F32),
             pltpu.VMEM((4, 128, F), BF16),
@@ -623,10 +693,10 @@
             pltpu.VMEM((4, T, F), BF16),
             pltpu.VMEM((T, F), BF16),
             pltpu.VMEM((4, T, F), F32),
-            pltpu.VMEM((16, F), F32),
-            pltpu.VMEM((16, F), F32),
-            pltpu.VMEM((NX, 16, F), F32),
-            pltpu.VMEM((NY, 16, F), F32),
+            pltpu.VMEM((8, F), F32),
+            pltpu.VMEM((8, F), F32),
+            pltpu.VMEM((NX, 8, F), F32),
+            pltpu.VMEM((NY, 8, F), F32),
             dma((4,)),
             dma((NZ,)),
             dma((3,)),
@@ -634,8 +704,8 @@
             dma((2, 4, 2)),
             dma((2, 5, 2)),
             dma((2, 5, 2)),
-            dma((3, NZ)),
-            dma((3, NZ)),
+            dma((5, NZ)),
+            dma((5, NZ)),
             dma((3,)),
             dma((3,)),
             dma((5, 2, 3)),
@@ -653,12 +723,19 @@
         branch_out,
         query_grads,
         query_weight,
-        norm_gain.reshape(1, F),
+        norm_gain.reshape(F // 128, 128),
         coef_weight.T,
         static_coef,
     )
-    so, bo, wo, gain, cwg, stat = outs
-    return so, bo, wo, gain.reshape(F), cwg.T, stat[0:6, 0:4].T
+    so, bo, wo, gain, cwg, stat = pl.pallas_call(
+        copy_kernel,
+        out_shape=[jax.ShapeDtypeStruct(o.shape, o.dtype) for o in outs],
+        in_specs=[any_spec] * 3 + [vmem] * 3,
+        out_specs=[any_spec] * 3 + [vmem] * 3,
+        scratch_shapes=[pltpu.VMEM(o.shape, o.dtype) for o in outs[:3]] + [dma((2, 12))],
+        compiler_params=pltpu.CompilerParams(vmem_limit_bytes=60 * 1024 * 1024),
+    )(*outs)
+    return so, bo, wo, gain.reshape(F), cwg.T, stat
 
 
 def solution(mesh):

time: 105 us -> 90.7 us (0.86)
  the two profiles are of different devices: /device:TPU:8 before, /device:TPU:1 now
where the time goes in v2:
time: 90.7 us; the launch traced here: 90.5 us
  Pallas kernels  89.8 us (99%)
    pallas_call x1, Pallas kernels, local(): pl.pallas_call(kernel, out_shape=(jax.ShapeDtypeStruct((4, T, F), BF16),...  86 us
    pallas_call x1, Pallas kernels, local(): pl.pallas_call(copy_kernel, out_shape=[jax.ShapeDtypeStruct(o.shape, o.dt...  3.86 us

profile of v2, /device:TPU:1, one launch (start us, length us, event | category | flops | bytes accessed | tf_op | source)
XLA Modules:
  0.0 90.5 jit_solution(12500958343414680773)
XLA Ops:
  0.6 86.0 %shard_map.127 = (bf16[4,256,640]{2,1,0:T(8,128)(2,1)}, bf16[256,640]{1,0:T(8,128)(2,1)}, f32[160,640]{1,0:T(8,128)}, f32[5,128]{1,0:T(8,128)}, f32[6,640]{1,0:T(8,128)}, /*index=5*/f32[4,6]{1,0:T(4,128)}) custom-call(bf16[4,256,640]{2,1,0:T(8,128)(2,1)} %s_h.1, bf16[4,256,640]{2,1,0:T(8,128)(2,1)} %g_h.1, bf16[256,640]{1,0:T(8,128)(2,1)} %b_h.1, ...), custom_call_target="tpu_custom_call" | custom-call | flops 8000000000 | bytes 13000000 | tf_op jit(solution)/shard_map/pallas_call | solution.py:654
  86.6 3.9 %shard_map.128 = (bf16[4,256,640]{2,1,0:T(8,128)(2,1)}, bf16[256,640]{1,0:T(8,128)(2,1)}, f32[160,640]{1,0:T(8,128)}, f32[5,128]{1,0:T(8,128)}, f32[6,640]{1,0:T(8,128)}, /*index=5*/f32[4,6]{1,0:T(4,128)}) custom-call(bf16[4,256,640]{2,1,0:T(8,128)(2,1)} %get-tuple-element.18.refs_0_, bf16[256,640]{1,0:T(8,128)(2,1)} %get-tuple-element.19.refs_1_, ...), custom_call_target="tpu_custom_call" | custom-call | tf_op jit(solution)/shard_map/pallas_call | solution.py:730

commit v3 on v2

--- a/solution.py
+++ b/solution.py
@@ -39,14 +39,14 @@
 
 def kernel(
     s_h, g_h, b_h, q_h, w_h, gain, cw, st,
-    so_h, bo_h, wo_h, gain_o, cw_o, st_o,
+    so_v, bo_v, wo_v, gain_o, cw_o, st_o,
     xs, gs, qq, wbuf,
     pbuf, rs_send, rs_recv,
     cl, r1, cfull, crit, crit_r, crit_f, hbuf,
     mixed, nts, nbuf, col1, colb, col2, cwx,
-    xsend, xrecv, keep, xa, wo_v,
-    so_v, bo_v, acc, sb, sc, sx, sy,
-    in_sem, win_sem, out_sem,
+    xsend, xrecv, keep, xa,
+    acc, sb, sc, sx, sy,
+    in_sem, win_sem,
     rs_ss, rs_rs, ag_ss, ag_rs, sync_ss, sync_rs, core_ss, core_rs, x_ss, x_rs, sm_ss, sm_rs,
 ):
     dp = lax.axis_index("dp")
@@ -261,6 +261,8 @@
         mix_inv = lax.rsqrt(mixed_sq / D + EPS)
         return proj, inv, sq, cf, wid, gw, mix_inv
 
+    rs_add(RIGHT, 1, 0)
+    rs_add(LEFT, 1, 1)
     for k in range(1, NZ):
         crit_back_in(k).wait_recv()
 
@@ -315,9 +317,6 @@
         n_swap(kk).start()
     for kk in range(2):
         nbuf[z, kk, core] = nts[pl.ds(pl.multiple_of((2 * kk + core) * RB, 32), RB), :]
-
-    rs_add(RIGHT, 1, 0)
-    rs_add(LEFT, 1, 1)
 
     def ag_copy(way, step, kk):
         blk = lax.rem(z - step + 1 + NZ, NZ) if way == RIGHT else lax.rem(z + step - 1, NZ)
@@ -470,22 +469,22 @@
         return gain_sum
 
     gain_part = norm(1)
+    gain_part = gain_part + norm(0)
+
+    def h_out(k):
+        return rcopy(hbuf.at[z], hbuf.at[z], sync_ss.at[2, k], sync_rs.at[2, k], zdev(k))
+
+    def h_in(k):
+        at = hbuf.at[lax.rem(z - k + NZ, NZ)]
+        return rcopy(at, at, sync_ss.at[2, k], sync_rs.at[2, k], zdev(k))
+
+    for k in range(1, NZ):
+        h_out(k).start()
     total = cl[z]
     for k in range(1, NZ):
         sync_out(k).wait_recv()
         total = total + r1[k]
     cfull[z] = total
-    gain_part = gain_part + norm(0)
-
-    def h_out(k):
-        return rcopy(hbuf.at[z], hbuf.at[z], sync_ss.at[2, k], sync_rs.at[2, k], zdev(k))
-
-    def h_in(k):
-        at = hbuf.at[lax.rem(z - k + NZ, NZ)]
-        return rcopy(at, at, sync_ss.at[2, k], sync_rs.at[2, k], zdev(k))
-
-    for k in range(1, NZ):
-        h_out(k).start()
     for k in range(1, NZ):
         sync_back(k).start()
 
@@ -576,16 +575,10 @@
     lax.fori_loop(T // 32, T // 16, out_rows, 0)
     colb[...] = jnp.concatenate([cf[j][0:1] for j in range(4)] + [jnp.zeros((124, T), F32)], axis=0).T
     lax.fori_loop(0, T // 32, branch, 0)
-    bo_out = pltpu.make_async_copy(bo_v, bo_h, out_sem.at[0])
-    bo_out.start()
-    so_out = pltpu.make_async_copy(so_v, so_h, out_sem.at[1])
-    so_out.start()
 
     top, low = red_finish(4, xa[y])
     wo_v[:HB] = top
     wo_v[HB:] = low
-    wo_out = pltpu.make_async_copy(wo_v, wo_h, out_sem.at[2])
-    wo_out.start()
 
     for k in (1, 2, 3):
         sm_y_in(k).wait_recv()
@@ -619,30 +612,14 @@
     for k in (1, 2, 3):
         sm_x(k).wait_send()
         sm_y(k).wait_send()
-    bo_out.wait()
-    so_out.wait()
-    wo_out.wait()
 
 
 def copy_kernel(*refs):
-    src, dst, held, sem = refs[:6], refs[6:12], refs[12:15], refs[15]
-    pieces = [(0, (i, pl.ds(h, T // 2))) for i in range(4) for h in (0, T // 2)]
-    pieces += [(1, (pl.ds(h, T // 2),)) for h in (0, T // 2)]
-    pieces += [(2, (pl.ds(h, HB),)) for h in (0, HB)]
-    loads = [
-        pltpu.make_async_copy(src[i].at[at], held[i].at[at], sem.at[0, n]) for n, (i, at) in enumerate(pieces)
-    ]
-    stores = [
-        pltpu.make_async_copy(held[i].at[at], dst[i].at[at], sem.at[1, n]) for n, (i, at) in enumerate(pieces)
-    ]
-    for c in loads:
+    src, dst, sem = refs[:6], refs[6:12], refs[12]
+    copies = [pltpu.make_async_copy(src[i], dst[i], sem.at[i]) for i in range(6)]
+    for c in copies:
         c.start()
-    for i in range(3, 6):
-        dst[i][...] = src[i][...]
-    for load, store in zip(loads, stores):
-        load.wait()
-        store.start()
-    for c in stores:
+    for c in copies:
         c.wait()
 
 
@@ -654,15 +631,15 @@
     outs = pl.pallas_call(
         kernel,
         out_shape=(
-            jax.ShapeDtypeStruct((4, T, F), BF16),
-            jax.ShapeDtypeStruct((T, F), BF16),
-            jax.ShapeDtypeStruct((RB, F), F32),
-            jax.ShapeDtypeStruct((F // 128, 128), F32),
-            jax.ShapeDtypeStruct((6, F), F32),
-            jax.ShapeDtypeStruct((4, 6), F32),
+            pltpu.VMEM((4, T, F), BF16),
+            pltpu.VMEM((T, F), BF16),
+            pltpu.VMEM((RB, F), F32),
+            pltpu.VMEM((F // 128, 128), F32),
+            pltpu.VMEM((6, F), F32),
+            pltpu.VMEM((4, 6), F32),
         ),
         in_specs=[any_spec] * 5 + [vmem, vmem, smem],
-        out_specs=(any_spec, any_spec, any_spec, vmem, vmem, vmem),
+        out_specs=(vmem,) * 6,
         scratch_shapes=[
             pltpu.VMEM((5, T, F), BF16),
             pltpu.VMEM((4, T, F), BF16),
@@ -689,9 +666,6 @@
             pltpu.VMEM((5, 2, 3, HB, F), BF16),
             pltpu.VMEM((5, 2, HB, F), F32),
             pltpu.VMEM((NY, RB, F), F32),
-            pltpu.VMEM((RB, F), F32),
-            pltpu.VMEM((4, T, F), BF16),
-            pltpu.VMEM((T, F), BF16),
             pltpu.VMEM((4, T, F), F32),
             pltpu.VMEM((8, F), F32),
             pltpu.VMEM((8, F), F32),
@@ -699,7 +673,6 @@
             pltpu.VMEM((NY, 8, F), F32),
             dma((4,)),
             dma((NZ,)),
-            dma((3,)),
             dma((2, 4, 2)),
             dma((2, 4, 2)),
             dma((2, 5, 2)),
@@ -730,10 +703,10 @@
     so, bo, wo, gain, cwg, stat = pl.pallas_call(
         copy_kernel,
         out_shape=[jax.ShapeDtypeStruct(o.shape, o.dtype) for o in outs],
-        in_specs=[any_spec] * 3 + [vmem] * 3,
-        out_specs=[any_spec] * 3 + [vmem] * 3,
-        scratch_shapes=[pltpu.VMEM(o.shape, o.dtype) for o in outs[:3]] + [dma((2, 12))],
-        compiler_params=pltpu.CompilerParams(vmem_limit_bytes=60 * 1024 * 1024),
+        in_specs=[any_spec] * 6,
+        out_specs=[any_spec] * 6,
+        scratch_shapes=[dma((6,))],
+        compiler_params=pltpu.CompilerParams(vmem_limit_bytes=1024 * 1024),
     )(*outs)
     return so, bo, wo, gain.reshape(F), cwg.T, stat
 

time: 90.7 us -> 85.7 us (0.945)
  Pallas kernels: 89.8 us -> 85 us
    pallas_call x1, Pallas kernels: 3.86 us -> 1.35 us  [local(): pl.pallas_call(copy_kernel, out_shape=[jax.ShapeDtypeStruct(o.shape, o.dt...]
    pallas_call x1, Pallas kernels: 86 us -> 83.6 us  [local(): pl.pallas_call(kernel, out_shape=(pltpu.VMEM((4, T, F), BF16), pltpu.VMEM...]
where the time goes in v3:
time: 85.7 us; the launch traced here: 85.6 us
  Pallas kernels  85 us (99%)
    pallas_call x1, Pallas kernels, local(): pl.pallas_call(kernel, out_shape=(pltpu.VMEM((4, T, F), BF16), pltpu.VMEM...  83.6 us

profile of v3, /device:TPU:1, one launch (start us, length us, event | category | flops | bytes accessed | tf_op | source)
XLA Modules:
  0.0 85.6 jit_solution(17254441135019203293)
XLA Ops:
  0.6 83.6 %shard_map.127 = (bf16[4,256,640]{2,1,0:T(8,128)(2,1)S(1)}, bf16[256,640]{1,0:T(8,128)(2,1)S(1)}, f32[160,640]{1,0:T(8,128)S(1)}, f32[5,128]{1,0:T(8,128)S(1)}, ...) custom-call(bf16[4,256,640]{2,1,0:T(8,128)(2,1)} %s_h.1, bf16[4,256,640]{2,1,0:T(8,128)(2,1)} %g_h.1, bf16[256,640]{1,0:T(8,128)(2,1)} %b_h.1, ...), custom_call_target="tpu_custom_call" | custom-call | flops 8000000000 | bytes 13000000 | tf_op jit(solution)/shard_map/pallas_call | solution.py:631
  84.3 1.4 %shard_map.128 = (bf16[4,256,640]{2,1,0:T(8,128)(2,1)}, bf16[256,640]{1,0:T(8,128)(2,1)}, f32[160,640]{1,0:T(8,128)}, f32[5,128]{1,0:T(8,128)}, f32[6,640]{1,0:T(8,128)}, /*index=5*/f32[4,6]{1,0:T(4,128)}) custom-call(bf16[4,256,640]{2,1,0:T(8,128)(2,1)S(1)} %get-tuple-element.18.refs_0_, bf16[256,640]{1,0:T(8,128)(2,1)S(1)} %get-tuple-element.19.refs_1_, ...), custom_call_target="tpu_custom_call" | custom-call | tf_op jit(solution)/shard_map/pallas_call | solution.py:703

commit v4 on v3

--- a/solution.py
+++ b/solution.py
@@ -201,8 +201,7 @@
         return rcopy(at, at, sync_ss.at[4, k], sync_rs.at[4, k], zdev(k))
 
     q_in.wait()
-    for k in (4, 3, 5):
-        rs_partial(k)
+    rs_partial(4)
 
     pl.semaphore_wait(barrier, len(peers))
     for k in range(1, NZ):
@@ -211,7 +210,8 @@
     rs_raw(LEFT, 0, 1)
     q_swap = rcopy(qq.at[core], qq.at[core], core_ss.at[0], core_rs.at[0], cdev)
     q_swap.start()
-    rs_partial(2)
+    rs_partial(3)
+    rs_partial(5)
     first = crit[z]
     for k in range(1, NZ):
         crit_out(k).wait_recv()
@@ -221,6 +221,8 @@
         crit_back(k).start()
     rs_raw(RIGHT, 1, 1)
     rs_raw(LEFT, 1, 0)
+    rs_partial(2)
+    rs_partial(6)
     g_in.wait()
     b_in.wait()
     lax.fori_loop(0, 2, gram_g, 0)
@@ -414,7 +416,6 @@
         bo_v[at, :] = v.astype(BF16)
         return carry
 
-    rs_partial(6)
     rs_add(RIGHT, 2, 1)
     rs_add(LEFT, 2, 0)
     for k in (1, 7, 0):
@@ -448,7 +449,6 @@
     ag_in(LEFT, 4, 1).wait_recv()
     pair_start(3)
     pair_finish(1)
-    pair_finish(2)
 
     def norm(blk):
         at = slice(blk * 128, blk * 128 + 128)
@@ -469,6 +469,8 @@
         return gain_sum
 
     gain_part = norm(1)
+    pair_finish(2)
+    red_forward(3)
     gain_part = gain_part + norm(0)
 
     def h_out(k):
@@ -488,7 +490,6 @@
     for k in range(1, NZ):
         sync_back(k).start()
 
-    red_forward(3)
     pair_finish(3)
     red_start(4, lambda r: xa[lax.rem(y + r, NY)])
 
@@ -520,7 +521,6 @@
         rows += [hi, mid, lo, wid[i], scale, cf[i][2:6], mix_inv, kfac]
         sums = jnp.broadcast_to(jnp.sum(cg, axis=1, keepdims=True), (8, 128))
         stat = stat + jnp.sum(jnp.where(lane8 == sub8 + 8 * i, sums, 0.0), axis=0, keepdims=True)
-    col2[...] = jnp.concatenate(rows, axis=0).T
     cpart = dot_nn(jnp.concatenate(left, axis=1).astype(BF16), xs[0:4].reshape(4 * T, F))
     cpart = cpart[0:8] + cpart[8:16] + cpart[16:24]
     last = jnp.concatenate([stat, jnp.zeros((1, F - 128), F32)], axis=1)
@@ -528,6 +528,7 @@
 
     sm_core = rcopy(sb, sc, sm_ss.at[0], sm_rs.at[0], cdev)
     sm_core.start()
+    col2[...] = jnp.concatenate(rows, axis=0).T
 
     lhs = col2[...].astype(BF16)
     for i in range(4):

time: 85.7 us -> 84.3 us (0.984)
  Pallas kernels: 85 us -> 83.5 us
    pallas_call x1, Pallas kernels: 83.6 us -> 82.1 us  [local(): pl.pallas_call(kernel, out_shape=(pltpu.VMEM((4, T, F), BF16), pltpu.VMEM...]
where the time goes in v4:
time: 84.3 us; the launch traced here: 84.1 us
  Pallas kernels  83.5 us (99%)
    pallas_call x1, Pallas kernels, local(): pl.pallas_call(kernel, out_shape=(pltpu.VMEM((4, T, F), BF16), pltpu.VMEM...  82.1 us

profile of v4, /device:TPU:1, one launch (start us, length us, event | category | flops | bytes accessed | tf_op | source)
XLA Modules:
  0.0 84.1 jit_solution(11202641878779454780)
XLA Ops:
  0.6 82.1 %shard_map.127 = (bf16[4,256,640]{2,1,0:T(8,128)(2,1)S(1)}, bf16[256,640]{1,0:T(8,128)(2,1)S(1)}, f32[160,640]{1,0:T(8,128)S(1)}, f32[5,128]{1,0:T(8,128)S(1)}, ...) custom-call(bf16[4,256,640]{2,1,0:T(8,128)(2,1)} %s_h.1, bf16[4,256,640]{2,1,0:T(8,128)(2,1)} %g_h.1, bf16[256,640]{1,0:T(8,128)(2,1)} %b_h.1, ...), custom_call_target="tpu_custom_call" | custom-call | flops 8000000000 | bytes 13000000 | tf_op jit(solution)/shard_map/pallas_call | solution.py:632
  82.8 1.4 %shard_map.128 = (bf16[4,256,640]{2,1,0:T(8,128)(2,1)}, bf16[256,640]{1,0:T(8,128)(2,1)}, f32[160,640]{1,0:T(8,128)}, f32[5,128]{1,0:T(8,128)}, f32[6,640]{1,0:T(8,128)}, /*index=5*/f32[4,6]{1,0:T(4,128)}) custom-call(bf16[4,256,640]{2,1,0:T(8,128)(2,1)S(1)} %get-tuple-element.18.refs_0_, bf16[256,640]{1,0:T(8,128)(2,1)S(1)} %get-tuple-element.19.refs_1_, ...), custom_call_target="tpu_custom_call" | custom-call | tf_op jit(solution)/shard_map/pallas_call | solution.py:704

commit v5 on v4

--- a/solution.py
+++ b/solution.py
@@ -148,7 +148,8 @@
         }
         proj = dot_nt(cw8, s_blk)
         for i in range(4):
-            cl[i, 0:7, at] = jnp.concatenate([proj[0:6, i * 128 : i * 128 + 128], gr[i, i]], axis=0)
+            p = proj[:, i * 128 : i * 128 + 128]
+            cl[2 * i, :, at] = jnp.concatenate([p[0:1], p[2:6]], axis=0)
         off = [gr[0, 1], gr[0, 2], gr[0, 3], gr[1, 2], gr[1, 3], gr[2, 3]]
         first = [proj[1:2, i * 128 : i * 128 + 128] for i in range(4)]
         first += [gr[i, i] for i in range(4)] + off + [jnp.zeros((1, 128), F32)] * 2
@@ -165,16 +166,10 @@
             [diag(sg[i * 128 : i * 128 + 128, j * 128 : j * 128 + 128]) for j in range(4)] for i in range(5)
         ]
         for i in range(4):
-            cl[i, 7:8, at] = route[4][i]
-        for half in range(2):
-            cl[4 + half, :, at] = jnp.concatenate(
-                [route[2 * half + i][j] for i in range(2) for j in range(4)], axis=0
-            )
+            cl[2 * i + 1, :, at] = jnp.concatenate([route[4][i]] + route[i], axis=0)
         return carry
 
     lax.fori_loop(0, 2, gram_s, 0)
-    for p in (6, 7):
-        cl[p] = jnp.zeros((8, T), F32)
 
     def sync_out(k):
         return rcopy(
@@ -246,8 +241,9 @@
             return crit_f[r // 2, r % 2 : r % 2 + 1]
 
         for i in range(4):
-            piece = cfull[i]
-            p8 = jnp.where(row8 < 6, piece, 0.0)
+            piece = cfull[2 * i]
+            first = crit_f[i // 2, i % 2 : i % 2 + 1]
+            p8 = jnp.concatenate([piece[0:1], first, piece[1:5], jnp.zeros((2, T), F32)], axis=0)
             iv = lax.rsqrt(g_of(i, i) / D + EPS)
             th = jnp.tanh(iv * p8)
             stc = jnp.zeros((8, T), F32)
@@ -511,8 +507,8 @@
     stat = jnp.zeros((1, 128), F32)
     for i in range(4):
         mix_grad = mix_inv * h8[i : i + 1] - kfac * gw[i]
-        route = cfull[4 + i // 2][4 * (i % 2) : 4 * (i % 2) + 4]
-        cg = jnp.concatenate([cfull[i][7:8], mix_grad, route, jnp.zeros((2, T), F32)], axis=0)
+        own = cfull[2 * i + 1]
+        cg = jnp.concatenate([own[0:1], mix_grad, own[1:5], jnp.zeros((2, T), F32)], axis=0)
         pre = cg * (1.0 - sq[i] * sq[i])
         pg = pre * inv[i]
         scale = jnp.sum(pre * proj[i], axis=0, keepdims=True) * (inv[i] * inv[i] * inv[i] / D)
@@ -649,9 +645,9 @@
             pltpu.VMEM((NZ, T, F), F32),
             pltpu.VMEM((2, 4, 2, T // 2, F), BF16),
             pltpu.VMEM((2, 4, 2, T // 2, F), BF16),
-            pltpu.VMEM((NZ, 8, T), F32),
-            pltpu.VMEM((NZ, 8, T), F32),
-            pltpu.VMEM((NZ, 8, T), F32),
+            pltpu.VMEM((NZ, 5, T), F32),
+            pltpu.VMEM((NZ, 5, T), F32),
+            pltpu.VMEM((NZ, 5, T), F32),
             pltpu.VMEM((NZ, 2, T), F32),
             pltpu.VMEM((NZ, 2, T), F32),
             pltpu.VMEM((NZ, 2, T), F32),

time: 84.3 us -> 84.2 us (level)
  no operation moved by 1% of the time
where the time goes in v5:
time: 84.2 us; the launch traced here: 84.1 us
  Pallas kernels  83.5 us (99%)
    pallas_call x1, Pallas kernels, local(): pl.pallas_call(kernel, out_shape=(pltpu.VMEM((4, T, F), BF16), pltpu.VMEM...  82.1 us

profile of v5, /device:TPU:1, one launch (start us, length us, event | category | flops | bytes accessed | tf_op | source)
XLA Modules:
  0.0 84.1 jit_solution(2365802612516840032)
XLA Ops:
  0.6 82.1 %shard_map.127 = (bf16[4,256,640]{2,1,0:T(8,128)(2,1)S(1)}, bf16[256,640]{1,0:T(8,128)(2,1)S(1)}, f32[160,640]{1,0:T(8,128)S(1)}, f32[5,128]{1,0:T(8,128)S(1)}, ...) custom-call(bf16[4,256,640]{2,1,0:T(8,128)(2,1)} %s_h.1, bf16[4,256,640]{2,1,0:T(8,128)(2,1)} %g_h.1, bf16[256,640]{1,0:T(8,128)(2,1)} %b_h.1, ...), custom_call_target="tpu_custom_call" | custom-call | flops 8000000000 | bytes 13000000 | tf_op jit(solution)/shard_map/pallas_call | solution.py:628
  82.8 1.4 %shard_map.128 = (bf16[4,256,640]{2,1,0:T(8,128)(2,1)}, bf16[256,640]{1,0:T(8,128)(2,1)}, f32[160,640]{1,0:T(8,128)}, f32[5,128]{1,0:T(8,128)}, f32[6,640]{1,0:T(8,128)}, /*index=5*/f32[4,6]{1,0:T(4,128)}) custom-call(bf16[4,256,640]{2,1,0:T(8,128)(2,1)S(1)} %get-tuple-element.18.refs_0_, bf16[256,640]{1,0:T(8,128)(2,1)S(1)} %get-tuple-element.19.refs_1_, ...), custom_call_target="tpu_custom_call" | custom-call | tf_op jit(solution)/shard_map/pallas_call | solution.py:700
